TPU v7x, 128 devices: a whole 4x4x4 slice. The times are simulated.
128 devices in a mesh: var: 16 (over y, x), tile: 8 (over z, core).
Axes of the slice: x: 4, y: 4, z: 4, core: 2. Of those that a mesh axis runs over, the one named last changes fastest.
Arguments:
- tokens: bfloat16 [96, 96, 64, 512], P(None, 'tile', 'var'), may hold values from -6 to 6
- latent_queries: bfloat16 [3, 512], replicated, may hold values from -6 to 6
- perc_query: bfloat16 [512, 512], replicated, may hold values from -0.25 to 0.25
- perc_key: bfloat16 [512, 512], replicated
- perc_value: bfloat16 [512, 512], replicated, may hold values from -0.25 to 0.25
- perc_out: bfloat16 [512, 512], replicated, may hold values from -0.25 to 0.25
- norm_gains: float32 [2, 512], replicated, may hold values from 0.1 to 1.9
- swin_query: bfloat16 [512, 512], replicated
- swin_keyvalue: bfloat16 [512, 1024], replicated, may hold values from -0.25 to 0.25
- swin_out: bfloat16 [512, 512], replicated, may hold values from -0.25 to 0.25
- mlp_up: bfloat16 [512, 2048], replicated, may hold values from -0.25 to 0.25
- mlp_down: bfloat16 [2048, 512], replicated, may hold values from -0.125 to 0.125
Outputs:
- encoded: bfloat16 [96, 96, 3, 512], P('var', 'tile')
All inputs are finite; a program needn't handle non-finite values.
Results may differ from a plain program's by a relative error of at most 0.04.
The roundings to bfloat16 on the way count: a program that leaves them out, or rounds other values in their place, can miss the bound.
Values may be sent and summed in bfloat16 or wider, within the bound.
A program may use at most 512 MiB of HBM per device.

v0:
```python
import math

import jax
import jax.numpy as jnp
from jax import lax
from jax.sharding import PartitionSpec as P

HEADS = 16
HD = 32
LATENT = 3
WLAT = 6


epsilon = 1e-05


def from_behind(array, axis, by):
    size = lax.axis_size(axis)
    return lax.ppermute(array, axis, [(i, (i + by) % size) for i in range(size)])


def layer_norm(values, gain_row):
    average = jnp.mean(values, axis=-1, keepdims=True)
    centred = values - average
    spread = jnp.mean(centred * centred, axis=-1, keepdims=True)
    return centred * lax.rsqrt(spread + epsilon) * gain_row


def probe_matrix(latent_queries, perc_query, perc_key):
    model_width = perc_key.shape[0]
    queries = jnp.dot(latent_queries, perc_query, preferred_element_type=jnp.float32)
    key_heads = perc_key.astype(jnp.float32).reshape(model_width, HEADS, HD)
    query_heads = queries.reshape(LATENT, HEADS, HD)
    key_probe = jnp.sum(key_heads[:, None, :, :] * query_heads[None, :, :, :], axis=-1)
    return (key_probe / math.sqrt(HD)).reshape(model_width, LATENT * HEADS).astype(jnp.bfloat16)


def partial_rows(token_rows, key_probe, value_heads):
    row_count, lon_count, group_count, level_count, model_width = token_rows.shape
    blocks = token_rows.reshape(
        row_count // WLAT, WLAT, lon_count, group_count, level_count, model_width
    )

    def one_block(block):
        scores = jnp.einsum("rcgtd,dk->rcgtk", block, key_probe, preferred_element_type=jnp.float32)
        maxima = jnp.max(scores, axis=3)
        exponent = jnp.exp(scores - maxima[:, :, :, None, :])
        totals = jnp.sum(exponent, axis=3)
        blended = jnp.einsum(
            "rcgtk,rcgtd->rcgkd",
            exponent.astype(jnp.bfloat16),
            block,
            preferred_element_type=jnp.float32,
        ).astype(jnp.bfloat16)
        blended = blended.reshape(WLAT, lon_count, group_count, LATENT, HEADS, model_width)
        numerators = jnp.einsum(
            "rcgjhd,dhe->rcgjhe", blended, value_heads, preferred_element_type=jnp.float32
        )
        return (maxima, totals, numerators)

    maxima, totals, numerators = lax.map(one_block, blocks)
    leading = (row_count, lon_count, group_count)
    return (
        maxima.reshape(leading + (LATENT, HEADS)),
        totals.reshape(leading + (LATENT, HEADS)),
        numerators.reshape(leading + (LATENT, HEADS, HD)),
    )


def finish_rows(numerator_sum, denominator, latent_queries, perc_out):
    row_count, lon_count = (numerator_sum.shape[0], numerator_sum.shape[1])
    shares = numerator_sum / denominator[..., None]
    attention = shares.astype(jnp.bfloat16).reshape(row_count, lon_count, LATENT, HEADS * HD)
    latent = latent_queries.astype(jnp.float32) + jnp.dot(
        attention, perc_out, preferred_element_type=jnp.float32
    )
    return latent.astype(jnp.bfloat16)


def swin_windows(
    windows, labels, norm_gains, swin_query, swin_keyvalue, swin_out, mlp_up, mlp_down
):
    window_count, length, model_width = windows.shape
    residual = windows.astype(jnp.float32)
    normed = layer_norm(residual, norm_gains[0]).astype(jnp.bfloat16)
    queries = jnp.dot(normed, swin_query, preferred_element_type=jnp.float32).astype(jnp.bfloat16)
    keyvals = jnp.dot(normed, swin_keyvalue, preferred_element_type=jnp.float32).astype(
        jnp.bfloat16
    )
    queries = queries.reshape(window_count, length, HEADS, HD)
    key_part = keyvals[..., :model_width].reshape(window_count, length, HEADS, HD)
    value_part = keyvals[..., model_width:].reshape(window_count, length, HEADS, HD)
    logits = jnp.einsum(
        "wqhe,wkhe->whqk", queries, key_part, preferred_element_type=jnp.float32
    ) / math.sqrt(HD)
    allowed = labels[:, :, None] == labels[:, None, :]
    logits = jnp.where(allowed[:, None, :, :], logits, -jnp.inf)
    row_max = jnp.max(logits, axis=-1, keepdims=True)
    exponent = jnp.exp(logits - row_max)
    probs = (exponent / jnp.sum(exponent, axis=-1, keepdims=True)).astype(jnp.bfloat16)
    mixed = jnp.einsum(
        "whqk,wkhe->wqhe", probs, value_part, preferred_element_type=jnp.float32
    ).astype(jnp.bfloat16)
    mixed = mixed.reshape(window_count, length, model_width)
    residual = residual + jnp.dot(mixed, swin_out, preferred_element_type=jnp.float32)
    normed_two = layer_norm(residual, norm_gains[1]).astype(jnp.bfloat16)
    hidden = jax.nn.gelu(
        jnp.dot(normed_two, mlp_up, preferred_element_type=jnp.float32), approximate=False
    ).astype(jnp.bfloat16)
    return (residual + jnp.dot(hidden, mlp_down, preferred_element_type=jnp.float32)).astype(
        jnp.bfloat16
    )


def body(
    tokens,
    latent_queries,
    perc_query,
    perc_key,
    perc_value,
    perc_out,
    norm_gains,
    swin_query,
    swin_keyvalue,
    swin_out,
    mlp_up,
    mlp_down,
):
    lat_rows, lon_cols, levels, model_width = tokens.shape
    groups = lax.axis_size("var")
    block_rows = lat_rows // groups
    half_lat = WLAT // 2
    half_lon = lon_cols // 2
    row_index = lax.axis_index("var")
    key_probe = probe_matrix(latent_queries, perc_query, perc_key)
    value_heads = perc_value.reshape(model_width, HEADS, HD)
    grouped = tokens.reshape(lat_rows, lon_cols, 1, levels, model_width)
    maxima, totals, numerators = partial_rows(grouped, key_probe, value_heads)
    maxima = maxima[:, :, 0]
    totals = totals[:, :, 0]
    numerators = numerators[:, :, 0]
    global_max = lax.pmax(maxima.astype(jnp.bfloat16), "var").astype(maxima.dtype)
    scales = jnp.exp(maxima - global_max)
    scaled_num = jnp.roll(numerators * scales[..., None], -half_lat, axis=0)
    scaled_total = jnp.roll(totals * scales, -half_lat, axis=0)
    numerator_sum, denominator = (
        lax.psum_scatter(scaled_num, "var", scatter_dimension=0, tiled=True),
        lax.psum_scatter(scaled_total, "var", scatter_dimension=0, tiled=True),
    )
    latent_block = finish_rows(numerator_sum, denominator, latent_queries, perc_out)
    following = from_behind(latent_block[:, :half_lon], "tile", -1)
    shifted = jnp.concatenate([latent_block[:, half_lon:], following], axis=1)
    window_count = block_rows // WLAT
    length = WLAT * lon_cols * LATENT
    windows = shifted.reshape(window_count, length, model_width)
    lat_index = row_index * block_rows + jnp.arange(block_rows, dtype=jnp.int32)
    wrapped = (lat_index >= lat_rows - half_lat).astype(jnp.int32)
    labels = jnp.broadcast_to(wrapped[:, None, None], (block_rows, lon_cols, LATENT)).reshape(
        window_count, length
    )
    result = swin_windows(
        windows, labels, norm_gains, swin_query, swin_keyvalue, swin_out, mlp_up, mlp_down
    )
    return result.reshape(block_rows, lon_cols, LATENT, model_width)


def solution(mesh):
    placed = (P(None, "tile", "var", None), P(), P(), P(), P(), P(), P(), P(), P(), P(), P(), P())
    return jax.shard_map(
        body, mesh=mesh, in_specs=placed, out_specs=P("var", "tile", None, None), check_vma=False
    )
```

profile of v0, /device:TPU:1, one launch (start us, length us, event | category | flops | bytes accessed | tf_op | source)
XLA Modules:
  0.0 552.2 jit_solution(13185081362212531527)
XLA Ops:
  6.6 7.2 %copy.111 = bf16[96,12,4,512]{3,1,2,0:T(8,128)(2,1)} copy(bf16[96,12,4,512]{3,2,1,0:T(4,128)(2,1)} %param.14) | data formatting | bytes 9437184 | tf_op args[0]
  16.1 2.1 copy.113
  18.1 120.0 %while.14 = (s32[]{:T(128)}, f32[16,6,12,1,48]{4,2,1,3,0:T(8,128)S(1)}, f32[16,6,12,1,48]{4,3,2,1,0:T(1,128)}, f32[16,6,12,1,3,16,32]{6,5,4,2,1,0,3:T(8,128)}, b...) while((s32[]{:T(128)}, ...), condition=%wide.region_4.5_spmd, body=%wide.region_1.4_spmd.sunk | while | flops 143375616 | bytes 13938825 | solution.py:61
  21.3 2.1 fusion.143
  23.4 2.3 copy_dynamic-update-slice_fusion.2
  28.8 2.1 fusion.143
  30.9 2.2 copy_dynamic-update-slice_fusion.2
  36.2 2.1 fusion.143
  38.3 2.3 copy_dynamic-update-slice_fusion.2
  43.7 2.1 fusion.143
  45.8 2.3 copy_dynamic-update-slice_fusion.2
  51.3 2.1 fusion.143
  53.4 2.3 copy_dynamic-update-slice_fusion.2
  58.8 2.1 fusion.143
  60.9 2.3 copy_dynamic-update-slice_fusion.2
  66.3 2.1 fusion.143
  68.4 2.2 copy_dynamic-update-slice_fusion.2
  73.8 2.1 fusion.143
  75.9 2.3 copy_dynamic-update-slice_fusion.2
  81.3 2.1 fusion.143
  83.4 2.2 copy_dynamic-update-slice_fusion.2
  88.8 2.1 fusion.143
  90.9 2.3 copy_dynamic-update-slice_fusion.2
  96.2 2.1 fusion.143
  98.3 2.3 copy_dynamic-update-slice_fusion.2
  103.8 2.1 fusion.143
  105.9 2.3 copy_dynamic-update-slice_fusion.2
  111.2 2.1 fusion.143
  113.3 2.3 copy_dynamic-update-slice_fusion.2
  118.8 2.1 fusion.143
  120.9 2.2 copy_dynamic-update-slice_fusion.2
  126.2 2.1 fusion.143
  128.3 2.3 copy_dynamic-update-slice_fusion.2
  133.8 2.1 fusion.143
  135.9 2.3 copy_dynamic-update-slice_fusion.2
  140.1 3.1 convert_element_type.108
  146.9 85.2 %all-reduce.2.cloned.1.call-done = bf16[96,12,3,16]{3,2,1,0:T(4,128)(2,1)} async-done(((bf16[96,12,3,16]{3,2,1,0:T(4,128)(2,1)}), bf16[96,12,3,16]{3,2,1,0:T(4,128)(2,1)}) %all-reduce.2.cloned.1.call-update) | async-done | bytes 110608 | tf_op jit(solution)/shard_map/pmax | solution.py:142
  232.2 3.9 fusion.106
  236.1 11.0 %bitcast_multiply_fusion = f32[96,12,3,16,32]{4,3,2,1,0:T(8,128)S(1)} fusion(f32[16,6,12,1,3,16,32]{6,5,4,2,1,0,3:T(8,128)} %get-tuple-element.44, f32[96,12,3,16]{3,2,1,0:T(4,128)S(1)} %get-tuple-element.104), kind=kLoop, calls=%fused_computation.18 | loop fusion | flops 1769472 | bytes 14376960 | tf_op jit(solution)/shard_map/mul | solution.py:144
  247.1 11.4 %slice.47 = f32[93,12,3,16,32]{4,3,2,1,0:T(8,128)} slice(f32[96,12,3,16,32]{4,3,2,1,0:T(8,128)S(1)} %bitcast_multiply_fusion), slice={[3:96], [0:12], [0:3], [0:16], [0:32]} | slice | bytes 13713408 | tf_op jit(solution)/shard_map/jit(_roll_static)/slice | solution.py:144
  258.5 6.1 %copy-done.1 = f32[96,12,3,16,32]{4,3,2,1,0:T(8,128)} copy-done((f32[96,12,3,16,32]{4,3,2,1,0:T(8,128)}, f32[96,12,3,16,32]{4,3,2,1,0:T(8,128)S(1)}, u32[]{:S(2)}) %copy-start.1) | copy-done | bytes 7077912
  268.5 20.9 %pad_maximum_fusion = f32[96,12,3,16,32]{4,3,2,1,0:T(8,128)} fusion(f32[3,12,3,16,32]{4,3,2,1,0:T(8,128)S(1)} %slice-done, f32[93,12,3,16,32]{4,3,2,1,0:T(8,128)} %slice.47), kind=kLoop, calls=%fused_computation.17 | loop fusion | flops 1769472 | bytes 14155776 | tf_op jit(solution)/shard_map/jit(_roll_static)/concatenate | solution.py:144
  290.4 51.0 %reduce-scatter.5.cloned.1.call-done = f32[6,12,3,16]{3,1,2,0:T(8,128)} async-done(((f32[96,12,3,16]{3,1,2,0:T(8,128)}), f32[6,12,3,16]{3,1,2,0:T(8,128)}) %reduce-scatter.5.cloned.1.call-update) | async-done | bytes 13840 | tf_op jit(solution)/shard_map/reduce_scatter | solution.py:148
  342.4 173.2 %reduce-scatter.3.cloned.1.call-done = f32[6,12,3,16,32]{4,3,2,1,0:T(8,128)} async-done(((f32[96,12,3,16,32]{4,3,2,1,0:T(8,128)}), f32[6,12,3,16,32]{4,3,2,1,0:T(8,128)}) %reduce-scatter.3.cloned.1.call-update) | async-done | bytes 442384 | tf_op jit(solution)/shard_map/reduce_scatter | solution.py:147
  520.7 4.0 collective-permute-done
  531.4 4.0 fusion.111
  535.4 2.5 fusion.30
  538.5 6.3 %fusion.31 = bf16[216,512]{1,0:T(8,128)(2,1)S(1)} fusion(f32[216,512]{1,0:T(8,128)S(1)} %get-tuple-element.118, bf16[2048,512]{1,0:T(8,128)(2,1)S(1)} %copy-done, bf16[512,2048]{1,0:T(8,128)(2,1)} %param.24, f32[512]{0:T(512)S(1)} %bitcast.92, f32[216]{0:T(256)S(1)} %add_rsqrt_fusion, f32[216]{0:T(256)S(1)} %broadcast_multiply_fusion.1), kind=kOutput, calls=%fused_computation.57 | convolution fusion | flops 935387136 | bytes 4861632 | tf_op jit(solution)/shard_map/dot_general | solution.py:110
  (203 shorter events, 76.0 us)
Async XLA Ops:
  6.5 532.0 %copy-start = (bf16[2048,512]{1,0:T(8,128)(2,1)S(1)}, bf16[2048,512]{1,0:T(8,128)(2,1)}, u32[]{:S(2)}) copy-start(bf16[2048,512]{1,0:T(8,128)(2,1)} %param.25) | copy-start | bytes 6291460
  6.5 225.6 %all-reduce.2.cloned.1.call-start = ((), (), s32[]{:S(2)}) async-start(), calls=%async_computation.2 | async-start | bytes 2359296 | tf_op jit(solution)/shard_map/pmax | solution.py:142
  6.5 7.2 %copy-start.5 = (bf16[512,512]{1,0:T(8,128)(2,1)S(1)}, bf16[512,512]{1,0:T(8,128)(2,1)}, u32[]{:S(2)}) copy-start(bf16[512,512]{1,0:T(8,128)(2,1)} %param.16) | copy-start | bytes 1572868
  6.6 7.2 %copy-start.8 = (bf16[3,512]{1,0:T(4,128)(2,1)S(1)}, bf16[3,512]{1,0:T(4,128)(2,1)}, u32[]{:S(2)}) copy-start(bf16[3,512]{1,0:T(4,128)(2,1)} %param.15) | copy-start | bytes 9220
  20.2 1.1 copy-start.6
  27.6 1.1 copy-start.6
  35.1 1.1 copy-start.6
  42.6 1.1 copy-start.6
  50.1 1.1 copy-start.6
  57.7 1.1 copy-start.6
  65.2 1.1 copy-start.6
  72.7 1.1 copy-start.6
  80.2 1.1 copy-start.6
  87.6 1.1 copy-start.6
  95.1 1.1 copy-start.6
  102.6 1.1 copy-start.6
  110.1 1.1 copy-start.6
  117.6 1.1 copy-start.6
  125.1 1.1 copy-start.6
  132.6 1.1 copy-start.6
  140.1 3.4 copy-start.2
  143.3 198.2 %reduce-scatter.5.cloned.1.call-start = ((), (), s32[]{:S(2)}) async-start(), calls=%async_computation.4 | async-start | bytes 2506752 | tf_op jit(solution)/shard_map/reduce_scatter | solution.py:148
  247.1 17.6 %copy-start.1 = (f32[96,12,3,16,32]{4,3,2,1,0:T(8,128)}, f32[96,12,3,16,32]{4,3,2,1,0:T(8,128)S(1)}, u32[]{:S(2)}) copy-start(f32[96,12,3,16,32]{4,3,2,1,0:T(8,128)S(1)} %bitcast_multiply_fusion) | copy-start | bytes 21233668
  267.3 1.2 slice-start
  267.3 248.3 %reduce-scatter.3.cloned.1.call-start = ((), (), s32[]{:S(2)}) async-start(), calls=%async_computation.3 | async-start | bytes 30081024 | tf_op jit(solution)/shard_map/reduce_scatter | solution.py:147
  517.6 3.1 copy-start.9
  520.1 4.6 collective-permute-start
  526.9 3.9 copy-start.4
  531.4 4.0 copy-start.7
  535.4 2.5 copy-start.3
Sparse Core Ops, SparseCore 0:
  143.4 88.7 all-reduce.1
  267.5 73.9 reduce-scatter.4
  345.3 170.2 reduce-scatter.2
where the time goes:
time: 553 us; the launch traced here: 552 us
  waiting for transfers between devices  314 us (57%)
  local copies, waits for them, and re-layouts  104 us (19%)
  matrix products  72.1 us (13%)
  other arithmetic  47 us (8%)
  between operations  13.4 us (2%)
    reduce_scatter x1, waiting for transfers between devices, body(): lax.psum_scatter(scaled_num, 'var', scatter_dimension=0, tiled=True)  173 us
    pmax x1, waiting for transfers between devices, body(): lax.pmax(maxima.astype(jnp.bfloat16), 'var').astype(maxima.dtype)  85.2 us
    reduce_scatter x1, waiting for transfers between devices, body(): lax.psum_scatter(scaled_total, 'var', scatter_dimension=0, tiled=True)  51 us
    dynamic_update_slice x48, local copies, waits for them, and re-layouts, partial_rows(): maxima, totals, numerators = lax.map(one_block, blocks)  46.9 us
    dot_general x16, matrix products, one_block(): jnp.einsum('rcgjhd,dhe->rcgjhe', blended, value_heads, preferred_element_...  33.5 us
    concatenate x1, other arithmetic, body(): scaled_num = jnp.roll(numerators * scales[..., None], -half_lat, axis=0)  20.9 us
    dot_general x16, matrix products, one_block(): jnp.einsum('rcgtk,rcgtd->rcgkd', exponent.astype(jnp.bfloat16), block, pr...  17.8 us
    unnamed x21, local copies, waits for them, and re-layouts  16.7 us
  transfers between devices with their start and end apart: 4, of which 4 were waited for; matrix products, arithmetic and copies ran while one was open for 5% of the time, Pallas kernels for 0%

commit v1 on v0

v1 whole, which is shorter than its diff:
```python
import functools
import math

import jax
import jax.numpy as jnp
from jax import lax
from jax.experimental import pallas as pl
from jax.experimental.pallas import tpu as pltpu
from jax.sharding import PartitionSpec as P

F32 = jnp.float32
BF16 = jnp.bfloat16
D = 512
HEADS = 16
HD = 32
LATENT = 3
LEVS = 4
WLAT = 6
HALF = 6
RING = 4
N_VAR = RING * RING
N_TILE = 8
FF = 2048
PATCHES = WLAT * HALF
PAD = 40
SENT = 48
ROWS = 2 * LATENT * PAD
STATS = 128
MESH = pl.DeviceIdType.MESH
epsilon = 1e-05


def last_by_last(a, b):
    return lax.dot_general(a, b, (((1,), (1,)), ((), ())), preferred_element_type=F32)


def dot(a, b):
    return jnp.dot(a, b, preferred_element_type=F32)


def layer_norm(values, gain_row):
    average = jnp.mean(values, axis=-1, keepdims=True)
    centred = values - average
    spread = jnp.mean(centred * centred, axis=-1, keepdims=True)
    return centred * lax.rsqrt(spread + epsilon) * gain_row


def split(values, terms):
    parts = []
    for _ in range(terms):
        part = values.astype(BF16)
        parts.append(part)
        values = values - part.astype(F32)
    return parts


def gather_kernel(
    tokens, w_pq, w_pk, w_pv, w_po, lq_ref,
    out_ref,
    buf, pq, pk, pv, po,
    kp_scr, ex_scr, s_scr, v_scr, p_scr, px_scr, sc_scr, snum, rnum, sstat, rstat, att_scr,
    w_sem, tok_send, tok_recv, num_send, num_recv, stat_send, stat_recv,
):
    var = lax.axis_index("var")
    tile = lax.axis_index("tile")
    y, x = var // RING, var % RING
    west = lax.rem(tile + N_TILE - 1, N_TILE)
    east = lax.rem(tile + 1, N_TILE)

    barrier = pltpu.get_barrier_semaphore()
    for d in range(1, RING):
        for there in (y * RING + lax.rem(x + d, RING), lax.rem(y + d, RING) * RING + x):
            pl.semaphore_signal(
                barrier, inc=1, device_id={"var": there, "tile": tile}, device_id_type=MESH
            )
    for d in range(RING):
        there = y * RING + lax.rem(x + d, RING)
        pl.semaphore_signal(
            barrier, inc=1, device_id={"var": there, "tile": east}, device_id_type=MESH
        )
    pl.semaphore_wait(barrier, 3 * RING - 2)

    def slot_of(half, k):
        return lax.rem((y if half == 0 else x) + 1 + k, RING)

    def send_piece(half, k):
        slot = slot_of(half, k)
        mine = x if half == 0 else y
        lon = HALF if half == 0 else 0
        for d in (1, 3, 2, 0):
            other = lax.rem(mine + d, RING)
            if half == 0:
                band, there = slot * RING + other, y * RING + other
            else:
                band, there = other * RING + slot, other * RING + x
            first = WLAT * band + WLAT // 2
            second = lax.rem(WLAT * band + WLAT, WLAT * N_VAR)
            for part, row in ((0, first), (1, second)):
                src = tokens.at[pl.ds(row, WLAT // 2), pl.ds(lon, HALF)]
                dst = buf.at[half, slot, mine, pl.ds(part * (WLAT // 2), WLAT // 2)]
                if d == 0:
                    pltpu.make_async_copy(src, dst, tok_recv.at[half, slot]).start()
                else:
                    pltpu.make_async_remote_copy(
                        src_ref=src,
                        dst_ref=dst,
                        send_sem=tok_send.at[half, slot],
                        recv_sem=tok_recv.at[half, slot],
                        device_id={"var": there, "tile": tile},
                        device_id_type=MESH,
                    ).start()

    for k in range(2):
        for half in range(2):
            send_piece(half, k)

    weights = ((w_pq, pq), (w_pk, pk), (w_pv, pv), (w_po, po))
    loads = [pltpu.make_async_copy(src, dst, w_sem.at[i]) for i, (src, dst) in enumerate(weights)]
    for load in loads:
        load.start()

    row = lax.broadcasted_iota(jnp.int32, (STATS, LATENT * D), 0)
    col = lax.broadcasted_iota(jnp.int32, (STATS, LATENT * D), 1)
    ex_scr[...] = jnp.where(
        row == (col >> 9) * HEADS + ((col & (D - 1)) >> 5), 1.0, 0.0
    ).astype(BF16)
    loads[0].wait()
    queries = dot(lq_ref[...], pq[...])
    head_row = lax.broadcasted_iota(jnp.int32, (HEADS, D), 0)
    head_col = lax.broadcasted_iota(jnp.int32, (HEADS, D), 1) >> 5
    spread = jnp.concatenate(
        [jnp.where(head_row == head_col, queries[j : j + 1], 0.0) for j in range(LATENT)]
        + [jnp.zeros((STATS - LATENT * HEADS, D), F32)],
        axis=0,
    )
    loads[1].wait()
    probe = sum(last_by_last(part, pk[...]) for part in split(spread, 3))
    kp_scr[...] = (probe / math.sqrt(HD)).astype(BF16)
    loads[2].wait()

    def work_piece(half, k):
        slot = slot_of(half, k)
        index = half * RING + k
        pltpu.make_async_copy(buf.at[half, slot], buf.at[half, slot], tok_recv.at[half, slot]).wait()
        rows = buf[half, slot].reshape(RING * PATCHES * LEVS, D)
        s_scr[...] = last_by_last(rows, kp_scr[...])
        values = dot(rows, pv[...])
        for lanes in range(D // 128):
            v_scr[lanes] = values[:, lanes * 128 : (lanes + 1) * 128]
        maxima, totals = [], []
        for src in range(RING):
            scores = [
                s_scr[pl.ds(src * PATCHES * LEVS + t, PATCHES, stride=LEVS), :]
                for t in range(LEVS)
            ]
            top = functools.reduce(jnp.maximum, scores)
            total = jnp.zeros_like(top)
            for t in range(LEVS):
                weight = jnp.exp(scores[t] - top)
                total = total + weight
                p_scr[pl.ds((src * LEVS + t) * PAD, PATCHES), :] = weight
            maxima.append(top)
            totals.append(total)
        top = functools.reduce(jnp.maximum, maxima)
        total = jnp.zeros_like(top)
        for src in range(RING):
            scale = jnp.exp(maxima[src] - top)
            total = total + totals[src] * scale
            sc_scr[pl.ds(src * PAD, PATCHES), :] = scale
        lane = lax.broadcasted_iota(jnp.int32, (PATCHES, STATS), 1)
        sstat[index, 0:PATCHES, :] = jnp.where(
            lane < STATS // 2, top, pltpu.roll(total, STATS // 2, 1)
        )
        px_scr[0 : RING * LEVS * PAD] = dot(p_scr[...].astype(BF16), ex_scr[...])
        px_scr[RING * LEVS * PAD :] = sum(dot(part, ex_scr[...]) for part in split(sc_scr[...], 2))
        for lanes in range(D // 128):
            at = lanes * 128
            sums = [jnp.zeros((PATCHES, 128), F32) for _ in range(LATENT)]
            for src in range(RING):
                inner = [jnp.zeros((PATCHES, 128), F32) for _ in range(LATENT)]
                for t in range(LEVS):
                    value = v_scr[lanes, pl.ds(src * PATCHES * LEVS + t, PATCHES, stride=LEVS), :]
                    for j in range(LATENT):
                        inner[j] += value * px_scr[
                            pl.ds((src * LEVS + t) * PAD, PATCHES), j * D + at : j * D + at + 128
                        ]
                for j in range(LATENT):
                    sums[j] += inner[j] * px_scr[
                        pl.ds((RING * LEVS + src) * PAD, PATCHES), j * D + at : j * D + at + 128
                    ]
            for j in range(LATENT):
                snum[index, 0:PATCHES, j * D + at : j * D + at + 128] = sums[j].astype(BF16)
        mine = y if half == 0 else x
        there = slot * RING + x if half == 0 else y * RING + slot
        for src, dst, send, recv in (
            (snum, rnum, num_send, num_recv), (sstat, rstat, stat_send, stat_recv)
        ):
            if half == 0 and k == RING - 1:
                pltpu.make_async_copy(src.at[index], dst.at[half, mine], recv.at[half]).start()
            else:
                pltpu.make_async_remote_copy(
                    src_ref=src.at[index],
                    dst_ref=dst.at[half, mine],
                    send_sem=send.at[index],
                    recv_sem=recv.at[half],
                    device_id={"var": there, "tile": tile if half == 0 else west},
                    device_id_type=MESH,
                ).start()

    for k in range(RING):
        for half in range(2):
            work_piece(half, k)
            if k + 2 < RING:
                send_piece(half, k + 2)

    lane = lax.broadcasted_iota(jnp.int32, (PAD, STATS), 1)
    inside = lax.broadcasted_iota(jnp.int32, (PAD, STATS), 0) < PATCHES
    for half in range(2):
        pltpu.make_async_copy(rnum.at[half], rnum.at[half], num_recv.at[half]).wait()
        pltpu.make_async_copy(rstat.at[half], rstat.at[half], stat_recv.at[half]).wait()
        stats = [rstat[half, src] for src in range(RING)]
        top = functools.reduce(jnp.maximum, stats)
        scales = [jnp.exp(stat - top) for stat in stats]
        denominator = sum(
            pltpu.roll(stat, STATS // 2, 1) * scale for stat, scale in zip(stats, scales)
        )
        keep = (lane < LATENT * HEADS) & inside
        for src in range(RING):
            sc_scr[pl.ds(src * PAD, PAD), :] = jnp.where(keep, scales[src] / denominator, 0.0)
        px_scr[0 : RING * PAD] = sum(dot(part, ex_scr[...]) for part in split(sc_scr[...], 3))
        inside_wide = lax.broadcasted_iota(jnp.int32, (PAD, D), 0) < PATCHES
        for j in range(LATENT):
            share = sum(
                rnum[half, src, :, j * D : (j + 1) * D].astype(F32)[:PAD]
                * px_scr[pl.ds(src * PAD, PAD), j * D : (j + 1) * D]
                for src in range(RING)
            )
            att_scr[pl.ds((half * LATENT + j) * PAD, PAD), :] = jnp.where(inside_wide, share, 0.0)

    loads[3].wait()
    latent = dot(att_scr[...].astype(BF16), po[...])
    start = jnp.concatenate(
        [
            jnp.broadcast_to(lq_ref[j : j + 1, :].astype(F32), (PAD, D))
            for _ in range(2)
            for j in range(LATENT)
        ],
        axis=0,
    )
    out_ref[...] = (start + latent).astype(BF16)

    for half in range(2):
        for k in range(RING):
            slot = slot_of(half, k)
            sent = buf.at[half, slot, pl.ds(0, RING - 1)]
            pltpu.make_async_copy(sent, sent, tok_send.at[half, slot]).wait()
            if half == 1 or k < RING - 1:
                index = half * RING + k
                pltpu.make_async_copy(snum.at[index], snum.at[index], num_send.at[index]).wait()
                pltpu.make_async_copy(sstat.at[index], sstat.at[index], stat_send.at[index]).wait()


def window_kernel(
    latent_ref, gains_ref, w_sq, w_skv, w_so, w_up, w_down, out_ref,
    sq, skv, so, up, down, vt_scr, mix_scr, turn_scr, w_sem,
):
    weights = ((w_sq, sq), (w_skv, skv), (w_so, so), (w_up, up), (w_down, down))
    loads = [pltpu.make_async_copy(src, dst, w_sem.at[i]) for i, (src, dst) in enumerate(weights)]
    for load in loads:
        load.start()
    var = lax.axis_index("var")
    residual = latent_ref[...].astype(F32)
    normed = layer_norm(residual, gains_ref[0:1, :]).astype(BF16)
    loads[0].wait()
    queries = dot(normed, sq[...]).astype(BF16)
    loads[1].wait()
    keyvals = dot(normed, skv[...])
    keys = keyvals[:, :D]
    vt_scr[...] = jnp.transpose(keyvals[:, D:]).astype(BF16)

    def place(shape, axis):
        index = lax.broadcasted_iota(jnp.int32, shape, axis)
        for b in range(2 * LATENT - 1, 0, -1):
            index = jnp.where(index >= b * PAD, index - b * PAD, index)
        return index

    key_at = place((ROWS, ROWS), 0)
    query_at = place((ROWS, ROWS), 1)
    cut = WLAT // 2 * HALF
    apart = (key_at >= cut) != (query_at >= cut)
    excluded = (key_at >= PATCHES) | (apart & (var == N_VAR - 1))
    bias = jnp.where(excluded, -jnp.inf, 0.0)
    lane_head = lax.broadcasted_iota(jnp.int32, (ROWS, 256), 1) >> 5
    for h in range(HEADS):
        at = h // 8 * 256
        key_part = jnp.where(lane_head == h % 8, keys[:, at : at + 256], 0.0).astype(BF16)
        logits = last_by_last(key_part, queries[:, at : at + 256]) / math.sqrt(HD) + bias
        exponent = jnp.exp(logits - jnp.max(logits, axis=0, keepdims=True))
        probs = (exponent / jnp.sum(exponent, axis=0, keepdims=True)).astype(BF16)
        mix_scr[h * HD : (h + 1) * HD, :] = dot(vt_scr[h * HD : (h + 1) * HD, :], probs)
    mixed = jnp.transpose(mix_scr[...]).astype(BF16)
    loads[2].wait()
    residual = residual + dot(mixed, so[...])
    normed = layer_norm(residual, gains_ref[1:2, :]).astype(BF16)
    loads[3].wait()
    loads[4].wait()
    chunk = 512
    for c in range(0, FF, chunk):
        wide = dot(normed, up[:, c : c + chunk])
        hidden = (0.5 * wide * (1.0 + lax.erf(wide * math.sqrt(0.5)))).astype(BF16)
        residual = residual + dot(hidden, down[c : c + chunk, :])
    lanes = D // 128
    for b in range(2 * LATENT):
        half, j = b // LATENT, b % LATENT
        for l in range(lanes):
            turn_scr[l, pl.ds(half * PATCHES * 4 + j, PATCHES, stride=4), :] = residual[
                b * PAD : b * PAD + PATCHES, l * 128 : (l + 1) * 128
            ]
    for half in range(2):
        for r in range(WLAT):
            for l in range(lanes):
                rows = turn_scr[l, pl.ds((half * PATCHES + r * HALF) * 4, HALF * 4), :]
                rows = rows.reshape(HALF, 4, 128)[:, :LATENT]
                out_ref[r, half * HALF : (half + 1) * HALF, :, l * 128 : (l + 1) * 128] = rows.astype(BF16)


def body(
    tokens, latent_queries, perc_query, perc_key, perc_value, perc_out, norm_gains, swin_query,
    swin_keyvalue, swin_out, mlp_up, mlp_down,
):
    whole = pl.BlockSpec(memory_space=pltpu.HBM)
    near = pl.BlockSpec(memory_space=pltpu.VMEM)
    matrices = (perc_query, perc_key, perc_value, perc_out)
    pairs = RING * LEVS * PAD
    latent = pl.pallas_call(
        gather_kernel,
        out_shape=jax.ShapeDtypeStruct((ROWS, D), BF16),
        in_specs=[whole] * (1 + len(matrices)) + [near],
        out_specs=near,
        scratch_shapes=[
            pltpu.VMEM((2, RING, RING, WLAT, HALF, LEVS, D), BF16),
            *[pltpu.VMEM(m.shape, m.dtype) for m in matrices],
            pltpu.VMEM((STATS, D), BF16),
            pltpu.VMEM((STATS, LATENT * D), BF16),
            pltpu.VMEM((RING * PATCHES * LEVS, STATS), F32),
            pltpu.VMEM((D // 128, RING * PATCHES * LEVS, 128), F32),
            pltpu.VMEM((pairs, STATS), F32),
            pltpu.VMEM((pairs + RING * PAD, LATENT * D), F32),
            pltpu.VMEM((RING * PAD, STATS), F32),
            pltpu.VMEM((2 * RING, SENT, LATENT * D), BF16),
            pltpu.VMEM((2, RING, SENT, LATENT * D), BF16),
            pltpu.VMEM((2 * RING, PAD, STATS), F32),
            pltpu.VMEM((2, RING, PAD, STATS), F32),
            pltpu.VMEM((ROWS, D), F32),
            pltpu.SemaphoreType.DMA((len(matrices),)),
            pltpu.SemaphoreType.DMA((2, RING)),
            pltpu.SemaphoreType.DMA((2, RING)),
            pltpu.SemaphoreType.DMA((2 * RING,)),
            pltpu.SemaphoreType.DMA((2,)),
            pltpu.SemaphoreType.DMA((2 * RING,)),
            pltpu.SemaphoreType.DMA((2,)),
        ],
        compiler_params=pltpu.CompilerParams(
            collective_id=0, has_side_effects=True, vmem_limit_bytes=113 * 512 * 1024
        ),
        cost_estimate=pl.CostEstimate(
            flops=8_000_000_000, bytes_accessed=100_000_000, transcendentals=0
        ),
    )(tokens, *matrices, latent_queries)
    block = (swin_query, swin_keyvalue, swin_out, mlp_up, mlp_down)
    return pl.pallas_call(
        window_kernel,
        out_shape=jax.ShapeDtypeStruct((WLAT, 2 * HALF, LATENT, D), BF16),
        in_specs=[near, near] + [whole] * len(block),
        out_specs=near,
        scratch_shapes=[
            *[pltpu.VMEM(m.shape, m.dtype) for m in block],
            pltpu.VMEM((D, ROWS), BF16),
            pltpu.VMEM((D, ROWS), F32),
            pltpu.VMEM((D // 128, 2 * PATCHES * 4, 128), F32),
            pltpu.SemaphoreType.DMA((len(block),)),
        ],
        compiler_params=pltpu.CompilerParams(vmem_limit_bytes=40 * 1024 * 1024),
        cost_estimate=pl.CostEstimate(
            flops=2_000_000_000, bytes_accessed=7_000_000, transcendentals=0
        ),
    )(latent, norm_gains, *block)


def solution(mesh):
    placed = (P(None, "tile", "var", None), P(), P(), P(), P(), P(), P(), P(), P(), P(), P(), P())
    return jax.shard_map(
        body, mesh=mesh, in_specs=placed, out_specs=P("var", "tile", None, None), check_vma=False
    )
```

time: 553 us -> 60.1 us (0.11)
  waiting for transfers between devices: 314 us -> 0 us
  local copies, waits for them, and re-layouts: 104 us -> 0.96 us
  matrix products: 72.1 us -> 0 us
  Pallas kernels: 0 us -> 58.7 us
  other arithmetic: 47 us -> 0 us
  between operations: 13.4 us -> 0.25 us
    reduce_scatter x2 -> x0, waiting for transfers between devices: 224 us -> none  [the longest x1 173 us: body(): lax.psum_scatter(scaled_num, 'var', scatter_dimension=0, tiled=True)]
    pmax x1 -> x0, waiting for transfers between devices: 85.2 us -> none  [body(): lax.pmax(maxima.astype(jnp.bfloat16), 'var').astype(maxima.dtype)]
    dot_general x55 -> x0, matrix products: 68.1 us -> none  [the longest x16 33.5 us: one_block(): jnp.einsum('rcgjhd,dhe->rcgjhe', blended, value_heads, preferred_element_...]
    pallas_call x0 -> x2, Pallas kernels: none -> 58.7 us  [the longest x1 50.9 us: body(): pl.pallas_call(gather_kernel, out_shape=jax.ShapeDtypeStruct((ROWS, D), B...]
    dynamic_update_slice x48 -> x0, local copies, waits for them, and re-layouts: 46.9 us -> none  [partial_rows(): maxima, totals, numerators = lax.map(one_block, blocks)]
    concatenate x2 -> x0, other arithmetic: 21.5 us -> none  [the longest x1 20.9 us: body(): scaled_num = jnp.roll(numerators * scales[..., None], -half_lat, axis=0)]
    reshape x18 -> x0, local copies, waits for them, and re-layouts: 18 us -> none
    unnamed x21 -> x14, local copies, waits for them, and re-layouts: 16.7 us -> 0.96 us
  transfers between devices with their start and end apart: 4 -> 0, of which waited for: 4 -> 0; matrix products, arithmetic and copies ran while one was open for 5% -> 0% of each run, Pallas kernels for 0% -> 0%
where the time goes in v1:
time: 60.1 us; the launch traced here: 60 us
  Pallas kernels  58.7 us (98%)
  local copies, waits for them, and re-layouts  0.96 us (2%)
    pallas_call x1, Pallas kernels, body(): pl.pallas_call(gather_kernel, out_shape=jax.ShapeDtypeStruct((ROWS, D), B...  50.9 us
    pallas_call x1, Pallas kernels, body(): pl.pallas_call(window_kernel, out_shape=jax.ShapeDtypeStruct((WLAT, 2 * H...  7.81 us

profile of v1, /device:TPU:1, one launch (start us, length us, event | category | flops | bytes accessed | tf_op | source)
XLA Modules:
  0.0 60.0 jit_solution(4749500967578443240)
XLA Ops:
  0.0 0.0 copy-start.1
  0.0 0.0 copy-start
  0.0 0.0 copy-start.4
  0.0 0.0 copy-start.2
  0.0 0.0 copy-start.3
  0.0 0.0 copy-start.5
  0.0 50.9 %shard_map.118.latent_ref = bf16[240,512]{1,0:T(8,128)(2,1)} custom-call(bf16[96,12,4,512]{3,2,1,0:T(4,128)(2,1)} %tokens.1, bf16[512,512]{1,0:T(8,128)(2,1)} %w_pq.1, bf16[512,512]{1,0:T(8,128)(2,1)} %w_pk.1, bf16[512,512]{1,0:T(8,128)(2,1)} %w_pv.1, bf16[512,512]{1,0:T(8,128)(2,1)} %w_po.1, bf16[3,512]{1,0:T(4,128)(2,1)} %lq_ref.1), custom_call_target="tpu_custom_call" | custom-call | flops 8000000000 | bytes 100000000 | tf_op jit(solution)/shard_map/pallas_call | solution.py:335
  51.0 0.0 copy-done.1
  51.0 0.0 copy-done
  51.0 0.0 copy-done.4
  51.0 0.0 copy-done.2
  51.0 0.0 copy-done.3
  51.0 0.0 copy-done.5
  51.0 0.0 copy-start.6
  51.0 0.9 %copy-done.6 = bf16[240,512]{1,0:T(8,128)(2,1)S(1)} copy-done((bf16[240,512]{1,0:T(8,128)(2,1)S(1)}, bf16[240,512]{1,0:T(8,128)(2,1)}, u32[]{:S(2)}) %copy-start.6) | copy-done | bytes 245784
  52.0 7.8 %shard_map.119 = bf16[6,12,3,512]{3,2,1,0:T(4,128)(2,1)} custom-call(bf16[240,512]{1,0:T(8,128)(2,1)S(1)} %copy-done.6, f32[2,512]{1,0:T(2,128)S(1)} %copy-done.5, bf16[512,512]{1,0:T(8,128)(2,1)S(1)} %copy-done.3, bf16[512,1024]{1,0:T(8,128)(2,1)S(1)} %copy-done.2, bf16[512,512]{1,0:T(8,128)(2,1)S(1)} %copy-done.4, bf16[512,2048]{1,0:T(8,128)(2,1)S(1)} %copy-done, ...), custom_call_target="tpu_custom_call" | custom-call | flops 2000000000 | bytes 7000000 | tf_op jit(solution)/shard_map/pallas_call | solution.py:371
Async XLA Ops:
  0.0 51.0 %copy-start.1 = (bf16[2048,512]{1,0:T(8,128)(2,1)S(1)}, bf16[2048,512]{1,0:T(8,128)(2,1)}, u32[]{:S(2)}) copy-start(bf16[2048,512]{1,0:T(8,128)(2,1)} %w_down.1) | copy-start | bytes 6291460
  0.0 51.0 %copy-start = (bf16[512,2048]{1,0:T(8,128)(2,1)S(1)}, bf16[512,2048]{1,0:T(8,128)(2,1)}, u32[]{:S(2)}) copy-start(bf16[512,2048]{1,0:T(8,128)(2,1)} %w_up.1) | copy-start | bytes 6291460
  0.0 51.0 %copy-start.4 = (bf16[512,512]{1,0:T(8,128)(2,1)S(1)}, bf16[512,512]{1,0:T(8,128)(2,1)}, u32[]{:S(2)}) copy-start(bf16[512,512]{1,0:T(8,128)(2,1)} %w_so.1) | copy-start | bytes 1572868
  0.0 51.0 %copy-start.2 = (bf16[512,1024]{1,0:T(8,128)(2,1)S(1)}, bf16[512,1024]{1,0:T(8,128)(2,1)}, u32[]{:S(2)}) copy-start(bf16[512,1024]{1,0:T(8,128)(2,1)} %w_skv.1) | copy-start | bytes 3145732
  0.0 51.0 %copy-start.3 = (bf16[512,512]{1,0:T(8,128)(2,1)S(1)}, bf16[512,512]{1,0:T(8,128)(2,1)}, u32[]{:S(2)}) copy-start(bf16[512,512]{1,0:T(8,128)(2,1)} %w_sq.1) | copy-start | bytes 1572868
  0.0 51.0 %copy-start.5 = (f32[2,512]{1,0:T(2,128)S(1)}, f32[2,512]{1,0:T(2,128)}, u32[]{:S(2)}) copy-start(f32[2,512]{1,0:T(2,128)} %gains_ref.1) | copy-start | bytes 12292
  51.0 0.9 %copy-start.6 = (bf16[240,512]{1,0:T(8,128)(2,1)S(1)}, bf16[240,512]{1,0:T(8,128)(2,1)}, u32[]{:S(2)}) copy-start(bf16[240,512]{1,0:T(8,128)(2,1)} %shard_map.118.latent_ref) | copy-start | bytes 737284

commit v2 on v1

--- a/solution.py
+++ b/solution.py
@@ -22,8 +22,9 @@
 N_TILE = 8
 FF = 2048
 PATCHES = WLAT * HALF
+BOTH = 2 * PATCHES
+GATHERED = 2 * BOTH * LEVS
 PAD = 40
-SENT = 48
 ROWS = 2 * LATENT * PAD
 STATS = 128
 MESH = pl.DeviceIdType.MESH
@@ -58,8 +59,10 @@
     tokens, w_pq, w_pk, w_pv, w_po, lq_ref,
     out_ref,
     buf, pq, pk, pv, po,
-    kp_scr, ex_scr, s_scr, v_scr, p_scr, px_scr, sc_scr, snum, rnum, sstat, rstat, att_scr,
+    kp_scr, ex_scr, s_scr, v_scr, p_scr, px_scr, sc_scr, keep, kstat, snum, rnum, sstat, rstat,
+    fnum, gnum, fstat, gstat, att_scr,
     w_sem, tok_send, tok_recv, num_send, num_recv, stat_send, stat_recv,
+    far_send, far_recv, fst_send, fst_recv,
 ):
     var = lax.axis_index("var")
     tile = lax.axis_index("tile")
@@ -68,37 +71,47 @@
     east = lax.rem(tile + 1, N_TILE)
 
     barrier = pltpu.get_barrier_semaphore()
-    for d in range(1, RING):
-        for there in (y * RING + lax.rem(x + d, RING), lax.rem(y + d, RING) * RING + x):
-            pl.semaphore_signal(
-                barrier, inc=1, device_id={"var": there, "tile": tile}, device_id_type=MESH
-            )
+
+    def greet(there, at):
+        pl.semaphore_signal(
+            barrier, inc=1, device_id={"var": there, "tile": at}, device_id_type=MESH
+        )
+
+    for d in (1, 3):
+        greet(y * RING + lax.rem(x + d, RING), tile)
+    for d in (1, 2, 3):
+        greet(lax.rem(y + d, RING) * RING + x, tile)
     for d in range(RING):
-        there = y * RING + lax.rem(x + d, RING)
-        pl.semaphore_signal(
-            barrier, inc=1, device_id={"var": there, "tile": east}, device_id_type=MESH
-        )
-    pl.semaphore_wait(barrier, 3 * RING - 2)
+        greet(y * RING + lax.rem(x + d, RING), east)
+    pl.semaphore_wait(barrier, 9)
 
     def slot_of(half, k):
         return lax.rem((y if half == 0 else x) + 1 + k, RING)
 
-    def send_piece(half, k):
+    def partners(half, slot):
+        a = x if half == 0 else y
+        odd = lax.rem(slot, 2)
+        one, three = a + 1 - 2 * lax.rem(a, 2), 3 - a
+        return one + odd * (three - one), three + odd * (one - three)
+
+    def along(half, place):
+        return y * RING + place if half == 0 else place * RING + x
+
+    def send_tokens(half, k):
         slot = slot_of(half, k)
-        mine = x if half == 0 else y
+        a = x if half == 0 else y
         lon = HALF if half == 0 else 0
-        for d in (1, 3, 2, 0):
-            other = lax.rem(mine + d, RING)
-            if half == 0:
-                band, there = slot * RING + other, y * RING + other
-            else:
-                band, there = other * RING + slot, other * RING + x
-            first = WLAT * band + WLAT // 2
-            second = lax.rem(WLAT * band + WLAT, WLAT * N_VAR)
-            for part, row in ((0, first), (1, second)):
+        first, second = partners(half, slot)
+        for which, src_at, owner in (
+            (0, 1, first), (1, 1, lax.rem(a + 2, RING)), (0, 0, a), (1, 0, second)
+        ):
+            band = slot * RING + owner if half == 0 else owner * RING + slot
+            upper = WLAT * band + WLAT // 2
+            lower = lax.rem(WLAT * band + WLAT, WLAT * N_VAR)
+            for part, row in ((0, upper), (1, lower)):
                 src = tokens.at[pl.ds(row, WLAT // 2), pl.ds(lon, HALF)]
-                dst = buf.at[half, slot, mine, pl.ds(part * (WLAT // 2), WLAT // 2)]
-                if d == 0:
+                dst = buf.at[half, slot, src_at, which, pl.ds(part * (WLAT // 2), WLAT // 2)]
+                if src_at == 0:
                     pltpu.make_async_copy(src, dst, tok_recv.at[half, slot]).start()
                 else:
                     pltpu.make_async_remote_copy(
@@ -106,13 +119,13 @@
                         dst_ref=dst,
                         send_sem=tok_send.at[half, slot],
                         recv_sem=tok_recv.at[half, slot],
-                        device_id={"var": there, "tile": tile},
+                        device_id={"var": along(half, first), "tile": tile},
                         device_id_type=MESH,
                     ).start()
 
     for k in range(2):
-        for half in range(2):
-            send_piece(half, k)
+        for half in (1, 0):
+            send_tokens(half, k)
 
     weights = ((w_pq, pq), (w_pk, pk), (w_pv, pv), (w_po, po))
     loads = [pltpu.make_async_copy(src, dst, w_sem.at[i]) for i, (src, dst) in enumerate(weights)]
@@ -138,69 +151,84 @@
     kp_scr[...] = (probe / math.sqrt(HD)).astype(BF16)
     loads[2].wait()
 
-    def work_piece(half, k):
+    lane = lax.broadcasted_iota(jnp.int32, (PAD, STATS), 1)
+    lane_wide = lax.broadcasted_iota(jnp.int32, (BOTH, STATS), 1)
+
+    def work(half, k):
         slot = slot_of(half, k)
         index = half * RING + k
         pltpu.make_async_copy(buf.at[half, slot], buf.at[half, slot], tok_recv.at[half, slot]).wait()
-        rows = buf[half, slot].reshape(RING * PATCHES * LEVS, D)
+        rows = buf[half, slot].reshape(GATHERED, D)
         s_scr[...] = last_by_last(rows, kp_scr[...])
         values = dot(rows, pv[...])
         for lanes in range(D // 128):
             v_scr[lanes] = values[:, lanes * 128 : (lanes + 1) * 128]
-        maxima, totals = [], []
-        for src in range(RING):
-            scores = [
-                s_scr[pl.ds(src * PATCHES * LEVS + t, PATCHES, stride=LEVS), :]
-                for t in range(LEVS)
-            ]
-            top = functools.reduce(jnp.maximum, scores)
-            total = jnp.zeros_like(top)
-            for t in range(LEVS):
-                weight = jnp.exp(scores[t] - top)
-                total = total + weight
-                p_scr[pl.ds((src * LEVS + t) * PAD, PATCHES), :] = weight
-            maxima.append(top)
-            totals.append(total)
-        top = functools.reduce(jnp.maximum, maxima)
+        members = [pl.ds(src * BOTH * LEVS + t, BOTH, stride=LEVS) for src in range(2) for t in range(LEVS)]
+        scores = [s_scr[member, :] for member in members]
+        top = functools.reduce(jnp.maximum, scores)
         total = jnp.zeros_like(top)
-        for src in range(RING):
-            scale = jnp.exp(maxima[src] - top)
-            total = total + totals[src] * scale
-            sc_scr[pl.ds(src * PAD, PATCHES), :] = scale
-        lane = lax.broadcasted_iota(jnp.int32, (PATCHES, STATS), 1)
-        sstat[index, 0:PATCHES, :] = jnp.where(
-            lane < STATS // 2, top, pltpu.roll(total, STATS // 2, 1)
-        )
-        px_scr[0 : RING * LEVS * PAD] = dot(p_scr[...].astype(BF16), ex_scr[...])
-        px_scr[RING * LEVS * PAD :] = sum(dot(part, ex_scr[...]) for part in split(sc_scr[...], 2))
+        for n, score in enumerate(scores):
+            weight = jnp.exp(score - top)
+            total = total + weight
+            p_scr[n * BOTH : (n + 1) * BOTH, :] = weight.astype(BF16)
+        stats = jnp.where(lane_wide < STATS // 2, top, pltpu.roll(total, STATS // 2, 1))
+        kstat[index, 0:PATCHES, :] = stats[:PATCHES]
+        sstat[index, 0:PATCHES, :] = stats[PATCHES:]
+        px_scr[...] = dot(p_scr[...], ex_scr[...])
         for lanes in range(D // 128):
             at = lanes * 128
-            sums = [jnp.zeros((PATCHES, 128), F32) for _ in range(LATENT)]
-            for src in range(RING):
-                inner = [jnp.zeros((PATCHES, 128), F32) for _ in range(LATENT)]
-                for t in range(LEVS):
-                    value = v_scr[lanes, pl.ds(src * PATCHES * LEVS + t, PATCHES, stride=LEVS), :]
-                    for j in range(LATENT):
-                        inner[j] += value * px_scr[
-                            pl.ds((src * LEVS + t) * PAD, PATCHES), j * D + at : j * D + at + 128
-                        ]
+            sums = [jnp.zeros((BOTH, 128), F32) for _ in range(LATENT)]
+            for n, member in enumerate(members):
+                value = v_scr[lanes, member, :]
                 for j in range(LATENT):
-                    sums[j] += inner[j] * px_scr[
-                        pl.ds((RING * LEVS + src) * PAD, PATCHES), j * D + at : j * D + at + 128
+                    sums[j] += value * px_scr[
+                        n * BOTH : (n + 1) * BOTH, j * D + at : j * D + at + 128
                     ]
             for j in range(LATENT):
-                snum[index, 0:PATCHES, j * D + at : j * D + at + 128] = sums[j].astype(BF16)
-        mine = y if half == 0 else x
-        there = slot * RING + x if half == 0 else y * RING + slot
+                keep[index, 0:PATCHES, j * D + at : j * D + at + 128] = sums[j][:PATCHES]
+                snum[index, 0:PATCHES, j * D + at : j * D + at + 128] = sums[j][PATCHES:].astype(BF16)
+        _, second = partners(half, slot)
         for src, dst, send, recv in (
             (snum, rnum, num_send, num_recv), (sstat, rstat, stat_send, stat_recv)
         ):
+            pltpu.make_async_remote_copy(
+                src_ref=src.at[index],
+                dst_ref=dst.at[index],
+                send_sem=send.at[index],
+                recv_sem=recv.at[index],
+                device_id={"var": along(half, second), "tile": tile},
+                device_id_type=MESH,
+            ).start()
+
+    def merge(half, k):
+        slot = slot_of(half, k)
+        index = half * RING + k
+        pltpu.make_async_copy(rstat.at[index], rstat.at[index], stat_recv.at[index]).wait()
+        mine, theirs = kstat[index], rstat[index]
+        top = jnp.maximum(mine, theirs)
+        my_scale, their_scale = jnp.exp(mine - top), jnp.exp(theirs - top)
+        total = (
+            pltpu.roll(mine, STATS // 2, 1) * my_scale
+            + pltpu.roll(theirs, STATS // 2, 1) * their_scale
+        )
+        fstat[index] = jnp.where(lane < STATS // 2, top, pltpu.roll(total, STATS // 2, 1))
+        scales = jnp.concatenate([my_scale, their_scale], axis=0)
+        scales = sum(dot(part, ex_scr[...]) for part in split(scales, 2))
+        pltpu.make_async_copy(rnum.at[index], rnum.at[index], num_recv.at[index]).wait()
+        fnum[index] = (
+            keep[index] * scales[:PAD] + rnum[index].astype(F32) * scales[PAD:]
+        ).astype(BF16)
+        source = y if half == 0 else x
+        there = slot * RING + x if half == 0 else y * RING + slot
+        for src, dst, send, recv in (
+            (fnum, gnum, far_send, far_recv), (fstat, gstat, fst_send, fst_recv)
+        ):
             if half == 0 and k == RING - 1:
-                pltpu.make_async_copy(src.at[index], dst.at[half, mine], recv.at[half]).start()
+                pltpu.make_async_copy(src.at[index], dst.at[half, source], recv.at[half]).start()
             else:
                 pltpu.make_async_remote_copy(
                     src_ref=src.at[index],
-                    dst_ref=dst.at[half, mine],
+                    dst_ref=dst.at[half, source],
                     send_sem=send.at[index],
                     recv_sem=recv.at[half],
                     device_id={"var": there, "tile": tile if half == 0 else west},
@@ -208,30 +236,33 @@
                 ).start()
 
     for k in range(RING):
-        for half in range(2):
-            work_piece(half, k)
+        for half in (1, 0):
+            work(half, k)
             if k + 2 < RING:
-                send_piece(half, k + 2)
-
-    lane = lax.broadcasted_iota(jnp.int32, (PAD, STATS), 1)
+                send_tokens(half, k + 2)
+            if k > 0:
+                merge(half, k - 1)
+    for half in (1, 0):
+        merge(half, RING - 1)
+
     inside = lax.broadcasted_iota(jnp.int32, (PAD, STATS), 0) < PATCHES
     for half in range(2):
-        pltpu.make_async_copy(rnum.at[half], rnum.at[half], num_recv.at[half]).wait()
-        pltpu.make_async_copy(rstat.at[half], rstat.at[half], stat_recv.at[half]).wait()
-        stats = [rstat[half, src] for src in range(RING)]
+        pltpu.make_async_copy(gnum.at[half], gnum.at[half], far_recv.at[half]).wait()
+        pltpu.make_async_copy(gstat.at[half], gstat.at[half], fst_recv.at[half]).wait()
+        stats = [gstat[half, src] for src in range(RING)]
         top = functools.reduce(jnp.maximum, stats)
         scales = [jnp.exp(stat - top) for stat in stats]
         denominator = sum(
             pltpu.roll(stat, STATS // 2, 1) * scale for stat, scale in zip(stats, scales)
         )
-        keep = (lane < LATENT * HEADS) & inside
+        valid = (lane < LATENT * HEADS) & inside
         for src in range(RING):
-            sc_scr[pl.ds(src * PAD, PAD), :] = jnp.where(keep, scales[src] / denominator, 0.0)
+            sc_scr[pl.ds(src * PAD, PAD), :] = jnp.where(valid, scales[src] / denominator, 0.0)
         px_scr[0 : RING * PAD] = sum(dot(part, ex_scr[...]) for part in split(sc_scr[...], 3))
         inside_wide = lax.broadcasted_iota(jnp.int32, (PAD, D), 0) < PATCHES
         for j in range(LATENT):
             share = sum(
-                rnum[half, src, :, j * D : (j + 1) * D].astype(F32)[:PAD]
+                gnum[half, src, :, j * D : (j + 1) * D].astype(F32)
                 * px_scr[pl.ds(src * PAD, PAD), j * D : (j + 1) * D]
                 for src in range(RING)
             )
@@ -252,12 +283,14 @@
     for half in range(2):
         for k in range(RING):
             slot = slot_of(half, k)
-            sent = buf.at[half, slot, pl.ds(0, RING - 1)]
+            index = half * RING + k
+            sent = buf.at[half, slot, 1]
             pltpu.make_async_copy(sent, sent, tok_send.at[half, slot]).wait()
+            pltpu.make_async_copy(snum.at[index], snum.at[index], num_send.at[index]).wait()
+            pltpu.make_async_copy(sstat.at[index], sstat.at[index], stat_send.at[index]).wait()
             if half == 1 or k < RING - 1:
-                index = half * RING + k
-                pltpu.make_async_copy(snum.at[index], snum.at[index], num_send.at[index]).wait()
-                pltpu.make_async_copy(sstat.at[index], sstat.at[index], stat_send.at[index]).wait()
+                pltpu.make_async_copy(fnum.at[index], fnum.at[index], far_send.at[index]).wait()
+                pltpu.make_async_copy(fstat.at[index], fstat.at[index], fst_send.at[index]).wait()
 
 
 def window_kernel(
@@ -331,33 +364,43 @@
     whole = pl.BlockSpec(memory_space=pltpu.HBM)
     near = pl.BlockSpec(memory_space=pltpu.VMEM)
     matrices = (perc_query, perc_key, perc_value, perc_out)
-    pairs = RING * LEVS * PAD
+    pieces = 2 * RING
     latent = pl.pallas_call(
         gather_kernel,
         out_shape=jax.ShapeDtypeStruct((ROWS, D), BF16),
         in_specs=[whole] * (1 + len(matrices)) + [near],
         out_specs=near,
         scratch_shapes=[
-            pltpu.VMEM((2, RING, RING, WLAT, HALF, LEVS, D), BF16),
+            pltpu.VMEM((2, RING, 2, 2, WLAT, HALF, LEVS, D), BF16),
             *[pltpu.VMEM(m.shape, m.dtype) for m in matrices],
             pltpu.VMEM((STATS, D), BF16),
             pltpu.VMEM((STATS, LATENT * D), BF16),
-            pltpu.VMEM((RING * PATCHES * LEVS, STATS), F32),
-            pltpu.VMEM((D // 128, RING * PATCHES * LEVS, 128), F32),
-            pltpu.VMEM((pairs, STATS), F32),
-            pltpu.VMEM((pairs + RING * PAD, LATENT * D), F32),
+            pltpu.VMEM((GATHERED, STATS), F32),
+            pltpu.VMEM((D // 128, GATHERED, 128), F32),
+            pltpu.VMEM((GATHERED, STATS), BF16),
+            pltpu.VMEM((GATHERED, LATENT * D), F32),
             pltpu.VMEM((RING * PAD, STATS), F32),
-            pltpu.VMEM((2 * RING, SENT, LATENT * D), BF16),
-            pltpu.VMEM((2, RING, SENT, LATENT * D), BF16),
-            pltpu.VMEM((2 * RING, PAD, STATS), F32),
+            pltpu.VMEM((pieces, PAD, LATENT * D), F32),
+            pltpu.VMEM((pieces, PAD, STATS), F32),
+            pltpu.VMEM((pieces, PAD, LATENT * D), BF16),
+            pltpu.VMEM((pieces, PAD, LATENT * D), BF16),
+            pltpu.VMEM((pieces, PAD, STATS), F32),
+            pltpu.VMEM((pieces, PAD, STATS), F32),
+            pltpu.VMEM((pieces, PAD, LATENT * D), BF16),
+            pltpu.VMEM((2, RING, PAD, LATENT * D), BF16),
+            pltpu.VMEM((pieces, PAD, STATS), F32),
             pltpu.VMEM((2, RING, PAD, STATS), F32),
             pltpu.VMEM((ROWS, D), F32),
             pltpu.SemaphoreType.DMA((len(matrices),)),
             pltpu.SemaphoreType.DMA((2, RING)),
             pltpu.SemaphoreType.DMA((2, RING)),
-            pltpu.SemaphoreType.DMA((2 * RING,)),
+            pltpu.SemaphoreType.DMA((pieces,)),
+            pltpu.SemaphoreType.DMA((pieces,)),
+            pltpu.SemaphoreType.DMA((pieces,)),
+            pltpu.SemaphoreType.DMA((pieces,)),
+            pltpu.SemaphoreType.DMA((pieces,)),
             pltpu.SemaphoreType.DMA((2,)),
-            pltpu.SemaphoreType.DMA((2 * RING,)),
+            pltpu.SemaphoreType.DMA((pieces,)),
             pltpu.SemaphoreType.DMA((2,)),
         ],
         compiler_params=pltpu.CompilerParams(

time: 60.1 us -> 56.1 us (0.933)
  Pallas kernels: 58.7 us -> 54.8 us
    pallas_call x1, Pallas kernels: 50.9 us -> 47 us  [body(): pl.pallas_call(gather_kernel, out_shape=jax.ShapeDtypeStruct((ROWS, D), B...]
where the time goes in v2:
time: 56.1 us; the launch traced here: 56 us
  Pallas kernels  54.8 us (98%)
  local copies, waits for them, and re-layouts  0.96 us (2%)
    pallas_call x1, Pallas kernels, body(): pl.pallas_call(gather_kernel, out_shape=jax.ShapeDtypeStruct((ROWS, D), B...  47 us
    pallas_call x1, Pallas kernels, body(): pl.pallas_call(window_kernel, out_shape=jax.ShapeDtypeStruct((WLAT, 2 * H...  7.81 us

profile of v2, /device:TPU:1, one launch (start us, length us, event | category | flops | bytes accessed | tf_op | source)
XLA Modules:
  0.0 56.0 jit_solution(2263934037666977975)
XLA Ops:
  0.0 0.0 copy-start.1
  0.0 0.0 copy-start
  0.0 0.0 copy-start.4
  0.0 0.0 copy-start.2
  0.0 0.0 copy-start.3
  0.0 0.0 copy-start.5
  0.0 47.0 %shard_map.118.latent_ref = bf16[240,512]{1,0:T(8,128)(2,1)} custom-call(bf16[96,12,4,512]{3,2,1,0:T(4,128)(2,1)} %tokens.1, bf16[512,512]{1,0:T(8,128)(2,1)} %w_pq.1, bf16[512,512]{1,0:T(8,128)(2,1)} %w_pk.1, bf16[512,512]{1,0:T(8,128)(2,1)} %w_pv.1, bf16[512,512]{1,0:T(8,128)(2,1)} %w_po.1, bf16[3,512]{1,0:T(4,128)(2,1)} %lq_ref.1), custom_call_target="tpu_custom_call" | custom-call | flops 8000000000 | bytes 100000000 | tf_op jit(solution)/shard_map/pallas_call | solution.py:368
  47.0 0.0 copy-done.1
  47.0 0.0 copy-done
  47.0 0.0 copy-done.4
  47.1 0.0 copy-done.2
  47.1 0.0 copy-done.3
  47.1 0.0 copy-done.5
  47.1 0.0 copy-start.6
  47.1 0.9 %copy-done.6 = bf16[240,512]{1,0:T(8,128)(2,1)S(1)} copy-done((bf16[240,512]{1,0:T(8,128)(2,1)S(1)}, bf16[240,512]{1,0:T(8,128)(2,1)}, u32[]{:S(2)}) %copy-start.6) | copy-done | bytes 245784
  48.0 7.8 %shard_map.119 = bf16[6,12,3,512]{3,2,1,0:T(4,128)(2,1)} custom-call(bf16[240,512]{1,0:T(8,128)(2,1)S(1)} %copy-done.6, f32[2,512]{1,0:T(2,128)S(1)} %copy-done.5, bf16[512,512]{1,0:T(8,128)(2,1)S(1)} %copy-done.3, bf16[512,1024]{1,0:T(8,128)(2,1)S(1)} %copy-done.2, bf16[512,512]{1,0:T(8,128)(2,1)S(1)} %copy-done.4, bf16[512,2048]{1,0:T(8,128)(2,1)S(1)} %copy-done, ...), custom_call_target="tpu_custom_call" | custom-call | flops 2000000000 | bytes 7000000 | tf_op jit(solution)/shard_map/pallas_call | solution.py:414
Async XLA Ops:
  0.0 47.0 %copy-start.1 = (bf16[2048,512]{1,0:T(8,128)(2,1)S(1)}, bf16[2048,512]{1,0:T(8,128)(2,1)}, u32[]{:S(2)}) copy-start(bf16[2048,512]{1,0:T(8,128)(2,1)} %w_down.1) | copy-start | bytes 6291460
  0.0 47.0 %copy-start = (bf16[512,2048]{1,0:T(8,128)(2,1)S(1)}, bf16[512,2048]{1,0:T(8,128)(2,1)}, u32[]{:S(2)}) copy-start(bf16[512,2048]{1,0:T(8,128)(2,1)} %w_up.1) | copy-start | bytes 6291460
  0.0 47.0 %copy-start.4 = (bf16[512,512]{1,0:T(8,128)(2,1)S(1)}, bf16[512,512]{1,0:T(8,128)(2,1)}, u32[]{:S(2)}) copy-start(bf16[512,512]{1,0:T(8,128)(2,1)} %w_so.1) | copy-start | bytes 1572868
  0.0 47.0 %copy-start.2 = (bf16[512,1024]{1,0:T(8,128)(2,1)S(1)}, bf16[512,1024]{1,0:T(8,128)(2,1)}, u32[]{:S(2)}) copy-start(bf16[512,1024]{1,0:T(8,128)(2,1)} %w_skv.1) | copy-start | bytes 3145732
  0.0 47.0 %copy-start.3 = (bf16[512,512]{1,0:T(8,128)(2,1)S(1)}, bf16[512,512]{1,0:T(8,128)(2,1)}, u32[]{:S(2)}) copy-start(bf16[512,512]{1,0:T(8,128)(2,1)} %w_sq.1) | copy-start | bytes 1572868
  0.0 47.0 %copy-start.5 = (f32[2,512]{1,0:T(2,128)S(1)}, f32[2,512]{1,0:T(2,128)}, u32[]{:S(2)}) copy-start(f32[2,512]{1,0:T(2,128)} %gains_ref.1) | copy-start | bytes 12292
  47.1 0.9 %copy-start.6 = (bf16[240,512]{1,0:T(8,128)(2,1)S(1)}, bf16[240,512]{1,0:T(8,128)(2,1)}, u32[]{:S(2)}) copy-start(bf16[240,512]{1,0:T(8,128)(2,1)} %shard_map.118.latent_ref) | copy-start | bytes 737284

commit v3 on v2

--- a/solution.py
+++ b/solution.py
@@ -61,7 +61,7 @@
     buf, pq, pk, pv, po,
     kp_scr, ex_scr, s_scr, v_scr, p_scr, px_scr, sc_scr, keep, kstat, snum, rnum, sstat, rstat,
     fnum, gnum, fstat, gstat, att_scr,
-    w_sem, tok_send, tok_recv, num_send, num_recv, stat_send, stat_recv,
+    w_sem, own_sem, tok_send, tok_recv, num_send, num_recv, stat_send, stat_recv,
     far_send, far_recv, fst_send, fst_recv,
 ):
     var = lax.axis_index("var")
@@ -83,7 +83,6 @@
         greet(lax.rem(y + d, RING) * RING + x, tile)
     for d in range(RING):
         greet(y * RING + lax.rem(x + d, RING), east)
-    pl.semaphore_wait(barrier, 9)
 
     def slot_of(half, k):
         return lax.rem((y if half == 0 else x) + 1 + k, RING)
@@ -97,22 +96,21 @@
     def along(half, place):
         return y * RING + place if half == 0 else place * RING + x
 
-    def send_tokens(half, k):
+    def send_tokens(half, k, own=False):
         slot = slot_of(half, k)
         a = x if half == 0 else y
         lon = HALF if half == 0 else 0
         first, second = partners(half, slot)
-        for which, src_at, owner in (
-            (0, 1, first), (1, 1, lax.rem(a + 2, RING)), (0, 0, a), (1, 0, second)
-        ):
+        for which, owner in ((0, a), (1, second)) if own else ((0, first), (1, lax.rem(a + 2, RING))):
+            src_at = 0 if own else 1
             band = slot * RING + owner if half == 0 else owner * RING + slot
             upper = WLAT * band + WLAT // 2
             lower = lax.rem(WLAT * band + WLAT, WLAT * N_VAR)
             for part, row in ((0, upper), (1, lower)):
                 src = tokens.at[pl.ds(row, WLAT // 2), pl.ds(lon, HALF)]
                 dst = buf.at[half, slot, src_at, which, pl.ds(part * (WLAT // 2), WLAT // 2)]
-                if src_at == 0:
-                    pltpu.make_async_copy(src, dst, tok_recv.at[half, slot]).start()
+                if own:
+                    pltpu.make_async_copy(src, dst, own_sem.at[half, slot]).start()
                 else:
                     pltpu.make_async_remote_copy(
                         src_ref=src,
@@ -123,14 +121,16 @@
                         device_id_type=MESH,
                     ).start()
 
-    for k in range(2):
-        for half in (1, 0):
-            send_tokens(half, k)
-
     weights = ((w_pq, pq), (w_pk, pk), (w_pv, pv), (w_po, po))
     loads = [pltpu.make_async_copy(src, dst, w_sem.at[i]) for i, (src, dst) in enumerate(weights)]
     for load in loads:
         load.start()
+    order = [(half, k) for k in range(RING) for half in (1, 0)]
+    for half, k in order:
+        send_tokens(half, k, own=True)
+    pl.semaphore_wait(barrier, 9)
+    for half, k in order[:4]:
+        send_tokens(half, k)
 
     row = lax.broadcasted_iota(jnp.int32, (STATS, LATENT * D), 0)
     col = lax.broadcasted_iota(jnp.int32, (STATS, LATENT * D), 1)
@@ -154,17 +154,29 @@
     lane = lax.broadcasted_iota(jnp.int32, (PAD, STATS), 1)
     lane_wide = lax.broadcasted_iota(jnp.int32, (BOTH, STATS), 1)
 
+    def products(half, k, src):
+        index = half * RING + k
+        rows = buf[half, slot_of(half, k), src].reshape(BOTH * LEVS, D)
+        at = src * BOTH * LEVS
+        s_scr[index, at : at + BOTH * LEVS, :] = last_by_last(rows, kp_scr[...])
+        values = dot(rows, pv[...])
+        for lanes in range(D // 128):
+            v_scr[index, lanes, at : at + BOTH * LEVS, :] = values[:, lanes * 128 : (lanes + 1) * 128]
+
     def work(half, k):
         slot = slot_of(half, k)
         index = half * RING + k
-        pltpu.make_async_copy(buf.at[half, slot], buf.at[half, slot], tok_recv.at[half, slot]).wait()
-        rows = buf[half, slot].reshape(GATHERED, D)
-        s_scr[...] = last_by_last(rows, kp_scr[...])
-        values = dot(rows, pv[...])
-        for lanes in range(D // 128):
-            v_scr[lanes] = values[:, lanes * 128 : (lanes + 1) * 128]
-        members = [pl.ds(src * BOTH * LEVS + t, BOTH, stride=LEVS) for src in range(2) for t in range(LEVS)]
-        scores = [s_scr[member, :] for member in members]
+        arrived = buf.at[half, slot, 1]
+        pltpu.make_async_copy(arrived, arrived, tok_recv.at[half, slot]).wait()
+        if k + 2 < RING:
+            send_tokens(half, k + 2)
+        products(half, k, 1)
+        members = [
+            pl.ds(src * BOTH * LEVS + t, BOTH, stride=LEVS)
+            for src in range(2)
+            for t in range(LEVS)
+        ]
+        scores = [s_scr[index, member, :] for member in members]
         top = functools.reduce(jnp.maximum, scores)
         total = jnp.zeros_like(top)
         for n, score in enumerate(scores):
@@ -174,19 +186,18 @@
         stats = jnp.where(lane_wide < STATS // 2, top, pltpu.roll(total, STATS // 2, 1))
         kstat[index, 0:PATCHES, :] = stats[:PATCHES]
         sstat[index, 0:PATCHES, :] = stats[PATCHES:]
-        px_scr[...] = dot(p_scr[...], ex_scr[...])
-        for lanes in range(D // 128):
-            at = lanes * 128
-            sums = [jnp.zeros((BOTH, 128), F32) for _ in range(LATENT)]
-            for n, member in enumerate(members):
-                value = v_scr[lanes, member, :]
-                for j in range(LATENT):
-                    sums[j] += value * px_scr[
-                        n * BOTH : (n + 1) * BOTH, j * D + at : j * D + at + 128
-                    ]
-            for j in range(LATENT):
-                keep[index, 0:PATCHES, j * D + at : j * D + at + 128] = sums[j][:PATCHES]
-                snum[index, 0:PATCHES, j * D + at : j * D + at + 128] = sums[j][PATCHES:].astype(BF16)
+        for at in range(0, LATENT * D, 256):
+            wide = dot(p_scr[...], ex_scr[:, at : at + 256])
+            for side in range(2):
+                lanes = (at % D) // 128 + side
+                here = sum(
+                    v_scr[index, lanes, member, :]
+                    * wide[n * BOTH : (n + 1) * BOTH, side * 128 : (side + 1) * 128]
+                    for n, member in enumerate(members)
+                )
+                columns = slice(at + side * 128, at + (side + 1) * 128)
+                keep[index, 0:PATCHES, columns] = here[:PATCHES]
+                snum[index, 0:PATCHES, columns] = here[PATCHES:].astype(BF16)
         _, second = partners(half, slot)
         for src, dst, send, recv in (
             (snum, rnum, num_send, num_recv), (sstat, rstat, stat_send, stat_recv)
@@ -235,13 +246,14 @@
                     device_id_type=MESH,
                 ).start()
 
-    for k in range(RING):
-        for half in (1, 0):
-            work(half, k)
-            if k + 2 < RING:
-                send_tokens(half, k + 2)
-            if k > 0:
-                merge(half, k - 1)
+    for half, k in order:
+        own = buf.at[half, slot_of(half, k), 0]
+        pltpu.make_async_copy(own, own, own_sem.at[half, slot_of(half, k)]).wait()
+        products(half, k, 0)
+    for half, k in order:
+        work(half, k)
+        if k > 0:
+            merge(half, k - 1)
     for half in (1, 0):
         merge(half, RING - 1)
 
@@ -375,10 +387,10 @@
             *[pltpu.VMEM(m.shape, m.dtype) for m in matrices],
             pltpu.VMEM((STATS, D), BF16),
             pltpu.VMEM((STATS, LATENT * D), BF16),
-            pltpu.VMEM((GATHERED, STATS), F32),
-            pltpu.VMEM((D // 128, GATHERED, 128), F32),
+            pltpu.VMEM((pieces, GATHERED, STATS), F32),
+            pltpu.VMEM((pieces, D // 128, GATHERED, 128), F32),
             pltpu.VMEM((GATHERED, STATS), BF16),
-            pltpu.VMEM((GATHERED, LATENT * D), F32),
+            pltpu.VMEM((RING * PAD, LATENT * D), F32),
             pltpu.VMEM((RING * PAD, STATS), F32),
             pltpu.VMEM((pieces, PAD, LATENT * D), F32),
             pltpu.VMEM((pieces, PAD, STATS), F32),
@@ -392,6 +404,7 @@
             pltpu.VMEM((2, RING, PAD, STATS), F32),
             pltpu.VMEM((ROWS, D), F32),
             pltpu.SemaphoreType.DMA((len(matrices),)),
+            pltpu.SemaphoreType.DMA((2, RING)),
             pltpu.SemaphoreType.DMA((2, RING)),
             pltpu.SemaphoreType.DMA((2, RING)),
             pltpu.SemaphoreType.DMA((pieces,)),

time: 56.1 us -> 55.5 us (0.989)
  Pallas kernels: 54.8 us -> 54.1 us
    pallas_call x1, Pallas kernels: 47 us -> 46.3 us  [body(): pl.pallas_call(gather_kernel, out_shape=jax.ShapeDtypeStruct((ROWS, D), B...]
where the time goes in v3:
time: 55.5 us; the launch traced here: 55.3 us
  Pallas kernels  54.1 us (97%)
  local copies, waits for them, and re-layouts  0.96 us (2%)
    pallas_call x1, Pallas kernels, body(): pl.pallas_call(gather_kernel, out_shape=jax.ShapeDtypeStruct((ROWS, D), B...  46.3 us
    pallas_call x1, Pallas kernels, body(): pl.pallas_call(window_kernel, out_shape=jax.ShapeDtypeStruct((WLAT, 2 * H...  7.81 us

profile of v3, /device:TPU:1, one launch (start us, length us, event | category | flops | bytes accessed | tf_op | source)
XLA Modules:
  0.0 55.3 jit_solution(6375255395806291276)
XLA Ops:
  0.0 0.0 copy-start.1
  0.0 0.0 copy-start
  0.0 0.0 copy-start.4
  0.0 0.0 copy-start.2
  0.0 0.0 copy-start.3
  0.0 0.0 copy-start.5
  0.0 46.3 %shard_map.118.latent_ref = bf16[240,512]{1,0:T(8,128)(2,1)} custom-call(bf16[96,12,4,512]{3,2,1,0:T(4,128)(2,1)} %tokens.1, bf16[512,512]{1,0:T(8,128)(2,1)} %w_pq.1, bf16[512,512]{1,0:T(8,128)(2,1)} %w_pk.1, bf16[512,512]{1,0:T(8,128)(2,1)} %w_pv.1, bf16[512,512]{1,0:T(8,128)(2,1)} %w_po.1, bf16[3,512]{1,0:T(4,128)(2,1)} %lq_ref.1), custom_call_target="tpu_custom_call" | custom-call | flops 8000000000 | bytes 100000000 | tf_op jit(solution)/shard_map/pallas_call | solution.py:380
  46.4 0.0 copy-done.1
  46.4 0.0 copy-done
  46.4 0.0 copy-done.4
  46.4 0.0 copy-done.2
  46.4 0.0 copy-done.3
  46.4 0.0 copy-done.5
  46.4 0.0 copy-start.6
  46.4 0.9 %copy-done.6 = bf16[240,512]{1,0:T(8,128)(2,1)S(1)} copy-done((bf16[240,512]{1,0:T(8,128)(2,1)S(1)}, bf16[240,512]{1,0:T(8,128)(2,1)}, u32[]{:S(2)}) %copy-start.6) | copy-done | bytes 245784
  47.4 7.8 %shard_map.119 = bf16[6,12,3,512]{3,2,1,0:T(4,128)(2,1)} custom-call(bf16[240,512]{1,0:T(8,128)(2,1)S(1)} %copy-done.6, f32[2,512]{1,0:T(2,128)S(1)} %copy-done.5, bf16[512,512]{1,0:T(8,128)(2,1)S(1)} %copy-done.3, bf16[512,1024]{1,0:T(8,128)(2,1)S(1)} %copy-done.2, bf16[512,512]{1,0:T(8,128)(2,1)S(1)} %copy-done.4, bf16[512,2048]{1,0:T(8,128)(2,1)S(1)} %copy-done, ...), custom_call_target="tpu_custom_call" | custom-call | flops 2000000000 | bytes 7000000 | tf_op jit(solution)/shard_map/pallas_call | solution.py:427
Async XLA Ops:
  0.0 46.4 %copy-start.1 = (bf16[2048,512]{1,0:T(8,128)(2,1)S(1)}, bf16[2048,512]{1,0:T(8,128)(2,1)}, u32[]{:S(2)}) copy-start(bf16[2048,512]{1,0:T(8,128)(2,1)} %w_down.1) | copy-start | bytes 6291460
  0.0 46.4 %copy-start = (bf16[512,2048]{1,0:T(8,128)(2,1)S(1)}, bf16[512,2048]{1,0:T(8,128)(2,1)}, u32[]{:S(2)}) copy-start(bf16[512,2048]{1,0:T(8,128)(2,1)} %w_up.1) | copy-start | bytes 6291460
  0.0 46.4 %copy-start.4 = (bf16[512,512]{1,0:T(8,128)(2,1)S(1)}, bf16[512,512]{1,0:T(8,128)(2,1)}, u32[]{:S(2)}) copy-start(bf16[512,512]{1,0:T(8,128)(2,1)} %w_so.1) | copy-start | bytes 1572868
  0.0 46.4 %copy-start.2 = (bf16[512,1024]{1,0:T(8,128)(2,1)S(1)}, bf16[512,1024]{1,0:T(8,128)(2,1)}, u32[]{:S(2)}) copy-start(bf16[512,1024]{1,0:T(8,128)(2,1)} %w_skv.1) | copy-start | bytes 3145732
  0.0 46.4 %copy-start.3 = (bf16[512,512]{1,0:T(8,128)(2,1)S(1)}, bf16[512,512]{1,0:T(8,128)(2,1)}, u32[]{:S(2)}) copy-start(bf16[512,512]{1,0:T(8,128)(2,1)} %w_sq.1) | copy-start | bytes 1572868
  0.0 46.4 %copy-start.5 = (f32[2,512]{1,0:T(2,128)S(1)}, f32[2,512]{1,0:T(2,128)}, u32[]{:S(2)}) copy-start(f32[2,512]{1,0:T(2,128)} %gains_ref.1) | copy-start | bytes 12292
  46.4 0.9 %copy-start.6 = (bf16[240,512]{1,0:T(8,128)(2,1)S(1)}, bf16[240,512]{1,0:T(8,128)(2,1)}, u32[]{:S(2)}) copy-start(bf16[240,512]{1,0:T(8,128)(2,1)} %shard_map.118.latent_ref) | copy-start | bytes 737284

commit v4 on v3

--- a/solution.py
+++ b/solution.py
@@ -46,6 +46,16 @@
     return centred * lax.rsqrt(spread + epsilon) * gain_row
 
 
+def gelu(x):
+    size = jnp.abs(x)
+    t = 1.0 / (1.0 + (0.3275911 * math.sqrt(0.5)) * size)
+    tail = 1.061405429
+    for term in (-1.453152027, 1.421413741, -0.284496736, 0.254829592):
+        tail = tail * t + term
+    tail = tail * t * jnp.exp2(x * x * (-0.5 * math.log2(math.e)))
+    return jnp.maximum(x, 0.0) - 0.5 * size * tail
+
+
 def split(values, terms):
     parts = []
     for _ in range(terms):
@@ -59,7 +69,7 @@
     tokens, w_pq, w_pk, w_pv, w_po, lq_ref,
     out_ref,
     buf, pq, pk, pv, po,
-    kp_scr, ex_scr, s_scr, v_scr, p_scr, px_scr, sc_scr, keep, kstat, snum, rnum, sstat, rstat,
+    kp_scr, ex_scr, s_scr, v_scr, s_nat, v_nat, p_scr, px_scr, sc_scr, keep, kstat, snum, rnum, sstat, rstat,
     fnum, gnum, fstat, gstat, att_scr,
     w_sem, own_sem, tok_send, tok_recv, num_send, num_recv, stat_send, stat_recv,
     far_send, far_recv, fst_send, fst_recv,
@@ -157,11 +167,16 @@
     def products(half, k, src):
         index = half * RING + k
         rows = buf[half, slot_of(half, k), src].reshape(BOTH * LEVS, D)
-        at = src * BOTH * LEVS
-        s_scr[index, at : at + BOTH * LEVS, :] = last_by_last(rows, kp_scr[...])
+        s_nat[...] = last_by_last(rows, kp_scr[...])
         values = dot(rows, pv[...])
         for lanes in range(D // 128):
-            v_scr[index, lanes, at : at + BOTH * LEVS, :] = values[:, lanes * 128 : (lanes + 1) * 128]
+            v_nat[lanes] = values[:, lanes * 128 : (lanes + 1) * 128]
+        for t in range(LEVS):
+            member = pl.ds(t, BOTH, stride=LEVS)
+            at = (src * LEVS + t) * BOTH
+            s_scr[index, at : at + BOTH, :] = s_nat[member, :]
+            for lanes in range(D // 128):
+                v_scr[index, at : at + BOTH, lanes * 128 : (lanes + 1) * 128] = v_nat[lanes, member, :]
 
     def work(half, k):
         slot = slot_of(half, k)
@@ -171,11 +186,7 @@
         if k + 2 < RING:
             send_tokens(half, k + 2)
         products(half, k, 1)
-        members = [
-            pl.ds(src * BOTH * LEVS + t, BOTH, stride=LEVS)
-            for src in range(2)
-            for t in range(LEVS)
-        ]
+        members = [slice(n * BOTH, (n + 1) * BOTH) for n in range(2 * LEVS)]
         scores = [s_scr[index, member, :] for member in members]
         top = functools.reduce(jnp.maximum, scores)
         total = jnp.zeros_like(top)
@@ -188,16 +199,11 @@
         sstat[index, 0:PATCHES, :] = stats[PATCHES:]
         for at in range(0, LATENT * D, 256):
             wide = dot(p_scr[...], ex_scr[:, at : at + 256])
-            for side in range(2):
-                lanes = (at % D) // 128 + side
-                here = sum(
-                    v_scr[index, lanes, member, :]
-                    * wide[n * BOTH : (n + 1) * BOTH, side * 128 : (side + 1) * 128]
-                    for n, member in enumerate(members)
-                )
-                columns = slice(at + side * 128, at + (side + 1) * 128)
-                keep[index, 0:PATCHES, columns] = here[:PATCHES]
-                snum[index, 0:PATCHES, columns] = here[PATCHES:].astype(BF16)
+            columns = slice(at, at + 256)
+            lanes = slice(at % D, at % D + 256)
+            here = sum(v_scr[index, member, lanes] * wide[member] for member in members)
+            keep[index, 0:PATCHES, columns] = here[:PATCHES]
+            snum[index, 0:PATCHES, columns] = here[PATCHES:].astype(BF16)
         _, second = partners(half, slot)
         for src, dst, send, recv in (
             (snum, rnum, num_send, num_recv), (sstat, rstat, stat_send, stat_recv)
@@ -306,13 +312,18 @@
 
 
 def window_kernel(
-    latent_ref, gains_ref, w_sq, w_skv, w_so, w_up, w_down, out_ref,
-    sq, skv, so, up, down, vt_scr, mix_scr, turn_scr, w_sem,
+    w_latent, gains_ref, w_sq, w_skv, w_so, w_up, w_down, out_ref,
+    latent_ref, sq, skv, so, up, down, vt_scr, mix_scr, turn_scr, w_sem,
 ):
-    weights = ((w_sq, sq), (w_skv, skv), (w_so, so), (w_up, up), (w_down, down))
-    loads = [pltpu.make_async_copy(src, dst, w_sem.at[i]) for i, (src, dst) in enumerate(weights)]
-    for load in loads:
+    weights = (
+        (w_latent, latent_ref), (w_sq, sq), (w_skv, skv), (w_so, so), (w_up, up), (w_down, down)
+    )
+    first, *loads = [
+        pltpu.make_async_copy(src, dst, w_sem.at[i]) for i, (src, dst) in enumerate(weights)
+    ]
+    for load in (first, *loads):
         load.start()
+    first.wait()
     var = lax.axis_index("var")
     residual = latent_ref[...].astype(F32)
     normed = layer_norm(residual, gains_ref[0:1, :]).astype(BF16)
@@ -339,9 +350,10 @@
     for h in range(HEADS):
         at = h // 8 * 256
         key_part = jnp.where(lane_head == h % 8, keys[:, at : at + 256], 0.0).astype(BF16)
-        logits = last_by_last(key_part, queries[:, at : at + 256]) / math.sqrt(HD) + bias
-        exponent = jnp.exp(logits - jnp.max(logits, axis=0, keepdims=True))
-        probs = (exponent / jnp.sum(exponent, axis=0, keepdims=True)).astype(BF16)
+        logits = last_by_last(key_part, queries[:, at : at + 256]) + bias
+        top = jnp.max(logits, axis=0, keepdims=True)
+        exponent = jnp.exp2((logits - top) * (math.log2(math.e) / math.sqrt(HD)))
+        probs = (exponent * (1.0 / jnp.sum(exponent, axis=0, keepdims=True))).astype(BF16)
         mix_scr[h * HD : (h + 1) * HD, :] = dot(vt_scr[h * HD : (h + 1) * HD, :], probs)
     mixed = jnp.transpose(mix_scr[...]).astype(BF16)
     loads[2].wait()
@@ -352,7 +364,7 @@
     chunk = 512
     for c in range(0, FF, chunk):
         wide = dot(normed, up[:, c : c + chunk])
-        hidden = (0.5 * wide * (1.0 + lax.erf(wide * math.sqrt(0.5)))).astype(BF16)
+        hidden = gelu(wide).astype(BF16)
         residual = residual + dot(hidden, down[c : c + chunk, :])
     lanes = D // 128
     for b in range(2 * LATENT):
@@ -388,7 +400,9 @@
             pltpu.VMEM((STATS, D), BF16),
             pltpu.VMEM((STATS, LATENT * D), BF16),
             pltpu.VMEM((pieces, GATHERED, STATS), F32),
-            pltpu.VMEM((pieces, D // 128, GATHERED, 128), F32),
+            pltpu.VMEM((pieces, GATHERED, D), F32),
+            pltpu.VMEM((BOTH * LEVS, STATS), F32),
+            pltpu.VMEM((D // 128, BOTH * LEVS, 128), F32),
             pltpu.VMEM((GATHERED, STATS), BF16),
             pltpu.VMEM((RING * PAD, LATENT * D), F32),
             pltpu.VMEM((RING * PAD, STATS), F32),
@@ -427,14 +441,15 @@
     return pl.pallas_call(
         window_kernel,
         out_shape=jax.ShapeDtypeStruct((WLAT, 2 * HALF, LATENT, D), BF16),
-        in_specs=[near, near] + [whole] * len(block),
+        in_specs=[whole, near] + [whole] * len(block),
         out_specs=near,
         scratch_shapes=[
+            pltpu.VMEM((ROWS, D), BF16),
             *[pltpu.VMEM(m.shape, m.dtype) for m in block],
             pltpu.VMEM((D, ROWS), BF16),
             pltpu.VMEM((D, ROWS), F32),
             pltpu.VMEM((D // 128, 2 * PATCHES * 4, 128), F32),
-            pltpu.SemaphoreType.DMA((len(block),)),
+            pltpu.SemaphoreType.DMA((1 + len(block),)),
         ],
         compiler_params=pltpu.CompilerParams(vmem_limit_bytes=40 * 1024 * 1024),
         cost_estimate=pl.CostEstimate(

time: 55.5 us -> 56.8 us (1.023)
  Pallas kernels: 54.1 us -> 55.4 us
    pallas_call x1, Pallas kernels: 7.81 us -> 9.1 us  [body(): pl.pallas_call(window_kernel, out_shape=jax.ShapeDtypeStruct((WLAT, 2 * H...]
where the time goes in v4:
time: 56.8 us; the launch traced here: 56.6 us
  Pallas kernels  55.4 us (98%)
  local copies, waits for them, and re-layouts  0.96 us (2%)
    pallas_call x1, Pallas kernels, body(): pl.pallas_call(gather_kernel, out_shape=jax.ShapeDtypeStruct((ROWS, D), B...  46.3 us
    pallas_call x1, Pallas kernels, body(): pl.pallas_call(window_kernel, out_shape=jax.ShapeDtypeStruct((WLAT, 2 * H...  9.1 us

profile of v4, /device:TPU:1, one launch (start us, length us, event | category | flops | bytes accessed | tf_op | source)
XLA Modules:
  0.0 56.6 jit_solution(14457717339259246618)
XLA Ops:
  0.0 0.0 copy-start.1
  0.0 0.0 copy-start
  0.0 0.0 copy-start.4
  0.0 0.0 copy-start.2
  0.0 0.0 copy-start.3
  0.0 0.0 copy-start.5
  0.0 46.3 %shard_map.118.w_latent = bf16[240,512]{1,0:T(8,128)(2,1)} custom-call(bf16[96,12,4,512]{3,2,1,0:T(4,128)(2,1)} %tokens.1, bf16[512,512]{1,0:T(8,128)(2,1)} %w_pq.1, bf16[512,512]{1,0:T(8,128)(2,1)} %w_pk.1, bf16[512,512]{1,0:T(8,128)(2,1)} %w_pv.1, bf16[512,512]{1,0:T(8,128)(2,1)} %w_po.1, bf16[3,512]{1,0:T(4,128)(2,1)} %lq_ref.1), custom_call_target="tpu_custom_call" | custom-call | flops 8000000000 | bytes 100000000 | tf_op jit(solution)/shard_map/pallas_call | solution.py:392
  46.4 0.0 copy-done.1
  46.4 0.0 copy-done
  46.4 0.0 copy-done.4
  46.4 0.0 copy-done.2
  46.4 0.0 copy-done.3
  46.4 0.0 copy-done.5
  46.4 0.0 copy-start.6
  46.4 0.9 %copy-done.6 = bf16[240,512]{1,0:T(8,128)(2,1)S(1)} copy-done((bf16[240,512]{1,0:T(8,128)(2,1)S(1)}, bf16[240,512]{1,0:T(8,128)(2,1)}, u32[]{:S(2)}) %copy-start.6) | copy-done | bytes 245784
  47.4 9.1 %shard_map.119 = bf16[6,12,3,512]{3,2,1,0:T(4,128)(2,1)} custom-call(bf16[240,512]{1,0:T(8,128)(2,1)S(1)} %copy-done.6, f32[2,512]{1,0:T(2,128)S(1)} %copy-done.5, bf16[512,512]{1,0:T(8,128)(2,1)S(1)} %copy-done.3, bf16[512,1024]{1,0:T(8,128)(2,1)S(1)} %copy-done.2, bf16[512,512]{1,0:T(8,128)(2,1)S(1)} %copy-done.4, bf16[512,2048]{1,0:T(8,128)(2,1)S(1)} %copy-done, ...), custom_call_target="tpu_custom_call" | custom-call | flops 2000000000 | bytes 7000000 | tf_op jit(solution)/shard_map/pallas_call | solution.py:441
Async XLA Ops:
  0.0 46.4 %copy-start.1 = (bf16[2048,512]{1,0:T(8,128)(2,1)S(1)}, bf16[2048,512]{1,0:T(8,128)(2,1)}, u32[]{:S(2)}) copy-start(bf16[2048,512]{1,0:T(8,128)(2,1)} %w_down.1) | copy-start | bytes 6291460
  0.0 46.4 %copy-start = (bf16[512,2048]{1,0:T(8,128)(2,1)S(1)}, bf16[512,2048]{1,0:T(8,128)(2,1)}, u32[]{:S(2)}) copy-start(bf16[512,2048]{1,0:T(8,128)(2,1)} %w_up.1) | copy-start | bytes 6291460
  0.0 46.4 %copy-start.4 = (bf16[512,512]{1,0:T(8,128)(2,1)S(1)}, bf16[512,512]{1,0:T(8,128)(2,1)}, u32[]{:S(2)}) copy-start(bf16[512,512]{1,0:T(8,128)(2,1)} %w_so.1) | copy-start | bytes 1572868
  0.0 46.4 %copy-start.2 = (bf16[512,1024]{1,0:T(8,128)(2,1)S(1)}, bf16[512,1024]{1,0:T(8,128)(2,1)}, u32[]{:S(2)}) copy-start(bf16[512,1024]{1,0:T(8,128)(2,1)} %w_skv.1) | copy-start | bytes 3145732
  0.0 46.4 %copy-start.3 = (bf16[512,512]{1,0:T(8,128)(2,1)S(1)}, bf16[512,512]{1,0:T(8,128)(2,1)}, u32[]{:S(2)}) copy-start(bf16[512,512]{1,0:T(8,128)(2,1)} %w_sq.1) | copy-start | bytes 1572868
  0.0 46.4 %copy-start.5 = (f32[2,512]{1,0:T(2,128)S(1)}, f32[2,512]{1,0:T(2,128)}, u32[]{:S(2)}) copy-start(f32[2,512]{1,0:T(2,128)} %gains_ref.1) | copy-start | bytes 12292
  46.4 0.9 %copy-start.6 = (bf16[240,512]{1,0:T(8,128)(2,1)S(1)}, bf16[240,512]{1,0:T(8,128)(2,1)}, u32[]{:S(2)}) copy-start(bf16[240,512]{1,0:T(8,128)(2,1)} %shard_map.118.w_latent) | copy-start | bytes 737284

commit v5 on v3

--- a/solution.py
+++ b/solution.py
@@ -135,7 +135,7 @@
     row = lax.broadcasted_iota(jnp.int32, (STATS, LATENT * D), 0)
     col = lax.broadcasted_iota(jnp.int32, (STATS, LATENT * D), 1)
     ex_scr[...] = jnp.where(
-        row == (col >> 9) * HEADS + ((col & (D - 1)) >> 5), 1.0, 0.0
+        (row & (STATS // 2 - 1)) == (col >> 9) * HEADS + ((col & (D - 1)) >> 5), 1.0, 0.0
     ).astype(BF16)
     loads[0].wait()
     queries = dot(lq_ref[...], pq[...])
@@ -152,6 +152,13 @@
     loads[2].wait()
 
     lane = lax.broadcasted_iota(jnp.int32, (PAD, STATS), 1)
+
+    def widen(scales):
+        head = scales.astype(BF16).astype(F32)
+        rest = pltpu.roll(scales - head, STATS // 2, 1)
+        low = lax.broadcasted_iota(jnp.int32, scales.shape, 1) < STATS // 2
+        return dot(jnp.where(low, head, rest).astype(BF16), ex_scr[...])
+
     lane_wide = lax.broadcasted_iota(jnp.int32, (BOTH, STATS), 1)
 
     def products(half, k, src):
@@ -163,14 +170,16 @@
         for lanes in range(D // 128):
             v_scr[index, lanes, at : at + BOTH * LEVS, :] = values[:, lanes * 128 : (lanes + 1) * 128]
 
-    def work(half, k):
+    def arrive(half, k):
         slot = slot_of(half, k)
-        index = half * RING + k
         arrived = buf.at[half, slot, 1]
         pltpu.make_async_copy(arrived, arrived, tok_recv.at[half, slot]).wait()
         if k + 2 < RING:
             send_tokens(half, k + 2)
-        products(half, k, 1)
+
+    def work(half, k):
+        slot = slot_of(half, k)
+        index = half * RING + k
         members = [
             pl.ds(src * BOTH * LEVS + t, BOTH, stride=LEVS)
             for src in range(2)
@@ -182,12 +191,12 @@
         for n, score in enumerate(scores):
             weight = jnp.exp(score - top)
             total = total + weight
-            p_scr[n * BOTH : (n + 1) * BOTH, :] = weight.astype(BF16)
+            p_scr[half, n * BOTH : (n + 1) * BOTH, :] = jnp.where(lane_wide < STATS // 2, weight, 0.0).astype(BF16)
         stats = jnp.where(lane_wide < STATS // 2, top, pltpu.roll(total, STATS // 2, 1))
         kstat[index, 0:PATCHES, :] = stats[:PATCHES]
         sstat[index, 0:PATCHES, :] = stats[PATCHES:]
         for at in range(0, LATENT * D, 256):
-            wide = dot(p_scr[...], ex_scr[:, at : at + 256])
+            wide = dot(p_scr[half], ex_scr[:, at : at + 256])
             for side in range(2):
                 lanes = (at % D) // 128 + side
                 here = sum(
@@ -224,7 +233,7 @@
         )
         fstat[index] = jnp.where(lane < STATS // 2, top, pltpu.roll(total, STATS // 2, 1))
         scales = jnp.concatenate([my_scale, their_scale], axis=0)
-        scales = sum(dot(part, ex_scr[...]) for part in split(scales, 2))
+        scales = widen(scales)
         pltpu.make_async_copy(rnum.at[index], rnum.at[index], num_recv.at[index]).wait()
         fnum[index] = (
             keep[index] * scales[:PAD] + rnum[index].astype(F32) * scales[PAD:]
@@ -250,10 +259,15 @@
         own = buf.at[half, slot_of(half, k), 0]
         pltpu.make_async_copy(own, own, own_sem.at[half, slot_of(half, k)]).wait()
         products(half, k, 0)
-    for half, k in order:
-        work(half, k)
-        if k > 0:
-            merge(half, k - 1)
+    for k in range(RING):
+        for half in (1, 0):
+            arrive(half, k)
+        for half in (1, 0):
+            products(half, k, 1)
+        for half in (1, 0):
+            work(half, k)
+            if k > 0:
+                merge(half, k - 1)
     for half in (1, 0):
         merge(half, RING - 1)
 
@@ -270,7 +284,7 @@
         valid = (lane < LATENT * HEADS) & inside
         for src in range(RING):
             sc_scr[pl.ds(src * PAD, PAD), :] = jnp.where(valid, scales[src] / denominator, 0.0)
-        px_scr[0 : RING * PAD] = sum(dot(part, ex_scr[...]) for part in split(sc_scr[...], 3))
+        px_scr[0 : RING * PAD] = widen(sc_scr[...])
         inside_wide = lax.broadcasted_iota(jnp.int32, (PAD, D), 0) < PATCHES
         for j in range(LATENT):
             share = sum(
@@ -339,9 +353,10 @@
     for h in range(HEADS):
         at = h // 8 * 256
         key_part = jnp.where(lane_head == h % 8, keys[:, at : at + 256], 0.0).astype(BF16)
-        logits = last_by_last(key_part, queries[:, at : at + 256]) / math.sqrt(HD) + bias
-        exponent = jnp.exp(logits - jnp.max(logits, axis=0, keepdims=True))
-        probs = (exponent / jnp.sum(exponent, axis=0, keepdims=True)).astype(BF16)
+        logits = last_by_last(key_part, queries[:, at : at + 256]) + bias
+        top = jnp.max(logits, axis=0, keepdims=True)
+        exponent = jnp.exp2((logits - top) * (math.log2(math.e) / math.sqrt(HD)))
+        probs = (exponent * (1.0 / jnp.sum(exponent, axis=0, keepdims=True))).astype(BF16)
         mix_scr[h * HD : (h + 1) * HD, :] = dot(vt_scr[h * HD : (h + 1) * HD, :], probs)
     mixed = jnp.transpose(mix_scr[...]).astype(BF16)
     loads[2].wait()
@@ -389,7 +404,7 @@
             pltpu.VMEM((STATS, LATENT * D), BF16),
             pltpu.VMEM((pieces, GATHERED, STATS), F32),
             pltpu.VMEM((pieces, D // 128, GATHERED, 128), F32),
-            pltpu.VMEM((GATHERED, STATS), BF16),
+            pltpu.VMEM((2, GATHERED, STATS), BF16),
             pltpu.VMEM((RING * PAD, LATENT * D), F32),
             pltpu.VMEM((RING * PAD, STATS), F32),
             pltpu.VMEM((pieces, PAD, LATENT * D), F32),
@@ -417,7 +432,7 @@
             pltpu.SemaphoreType.DMA((2,)),
         ],
         compiler_params=pltpu.CompilerParams(
-            collective_id=0, has_side_effects=True, vmem_limit_bytes=113 * 512 * 1024
+            collective_id=0, has_side_effects=True, vmem_limit_bytes=107 * 512 * 1024
         ),
         cost_estimate=pl.CostEstimate(
             flops=8_000_000_000, bytes_accessed=100_000_000, transcendentals=0

time: 55.5 us -> 53.7 us (0.968)
  Pallas kernels: 54.1 us -> 52.5 us
    pallas_call x1, Pallas kernels: 46.3 us -> 44.7 us  [body(): pl.pallas_call(gather_kernel, out_shape=jax.ShapeDtypeStruct((ROWS, D), B...]
where the time goes in v5:
time: 53.7 us; the launch traced here: 53.6 us
  Pallas kernels  52.5 us (98%)
  local copies, waits for them, and re-layouts  0.85 us (2%)
    pallas_call x1, Pallas kernels, body(): pl.pallas_call(gather_kernel, out_shape=jax.ShapeDtypeStruct((ROWS, D), B...  44.7 us
    pallas_call x1, Pallas kernels, body(): pl.pallas_call(window_kernel, out_shape=jax.ShapeDtypeStruct((WLAT, 2 * H...  7.77 us

profile of v5, /device:TPU:1, one launch (start us, length us, event | category | flops | bytes accessed | tf_op | source)
XLA Modules:
  0.0 53.6 jit_solution(9039914808627864387)
XLA Ops:
  0.0 0.0 copy-start.1
  0.0 0.0 copy-start
  0.0 0.0 copy-start.4
  0.0 0.0 copy-start.2
  0.0 0.0 copy-start.3
  0.0 0.0 copy-start.5
  0.0 0.8 %copy-done.5 = bf16[3,512]{1,0:T(4,128)(2,1)S(1)} copy-done((bf16[3,512]{1,0:T(4,128)(2,1)S(1)}, bf16[3,512]{1,0:T(4,128)(2,1)}, u32[]{:S(2)}) %copy-start.5) | copy-done | bytes 3096
  0.9 0.0 copy-start.6
  0.9 44.7 %shard_map.118.latent_ref = bf16[240,512]{1,0:T(8,128)(2,1)S(1)} custom-call(bf16[96,12,4,512]{3,2,1,0:T(4,128)(2,1)} %tokens.1, bf16[512,512]{1,0:T(8,128)(2,1)} %w_pq.1, bf16[512,512]{1,0:T(8,128)(2,1)} %w_pk.1, bf16[512,512]{1,0:T(8,128)(2,1)} %w_pv.1, bf16[512,512]{1,0:T(8,128)(2,1)} %w_po.1, bf16[3,512]{1,0:T(4,128)(2,1)S(1)} %copy-done.5), custom_call_target="tpu_custom_call" | custom-call | flops 8000000000 | bytes 100000000 | tf_op jit(solution)/shard_map/pallas_call | solution.py:395
  45.6 0.0 copy-done.1
  45.6 0.0 copy-done
  45.6 0.0 copy-done.4
  45.6 0.0 copy-done.2
  45.6 0.0 copy-done.3
  45.6 0.0 copy-done.6
  45.6 7.8 %shard_map.119 = bf16[6,12,3,512]{3,2,1,0:T(4,128)(2,1)} custom-call(bf16[240,512]{1,0:T(8,128)(2,1)S(1)} %shard_map.118.latent_ref, f32[2,512]{1,0:T(2,128)S(1)} %copy-done.6, bf16[512,512]{1,0:T(8,128)(2,1)S(1)} %copy-done.3, bf16[512,1024]{1,0:T(8,128)(2,1)S(1)} %copy-done.2, bf16[512,512]{1,0:T(8,128)(2,1)S(1)} %copy-done.4, ...), custom_call_target="tpu_custom_call" | custom-call | flops 2000000000 | bytes 7000000 | tf_op jit(solution)/shard_map/pallas_call | solution.py:442
Async XLA Ops:
  0.0 45.6 %copy-start.1 = (bf16[2048,512]{1,0:T(8,128)(2,1)S(1)}, bf16[2048,512]{1,0:T(8,128)(2,1)}, u32[]{:S(2)}) copy-start(bf16[2048,512]{1,0:T(8,128)(2,1)} %w_down.1) | copy-start | bytes 6291460
  0.0 45.6 %copy-start = (bf16[512,2048]{1,0:T(8,128)(2,1)S(1)}, bf16[512,2048]{1,0:T(8,128)(2,1)}, u32[]{:S(2)}) copy-start(bf16[512,2048]{1,0:T(8,128)(2,1)} %w_up.1) | copy-start | bytes 6291460
  0.0 45.6 %copy-start.4 = (bf16[512,512]{1,0:T(8,128)(2,1)S(1)}, bf16[512,512]{1,0:T(8,128)(2,1)}, u32[]{:S(2)}) copy-start(bf16[512,512]{1,0:T(8,128)(2,1)} %w_so.1) | copy-start | bytes 1572868
  0.0 45.6 %copy-start.2 = (bf16[512,1024]{1,0:T(8,128)(2,1)S(1)}, bf16[512,1024]{1,0:T(8,128)(2,1)}, u32[]{:S(2)}) copy-start(bf16[512,1024]{1,0:T(8,128)(2,1)} %w_skv.1) | copy-start | bytes 3145732
  0.0 45.6 %copy-start.3 = (bf16[512,512]{1,0:T(8,128)(2,1)S(1)}, bf16[512,512]{1,0:T(8,128)(2,1)}, u32[]{:S(2)}) copy-start(bf16[512,512]{1,0:T(8,128)(2,1)} %w_sq.1) | copy-start | bytes 1572868
  0.0 0.8 %copy-start.5 = (bf16[3,512]{1,0:T(4,128)(2,1)S(1)}, bf16[3,512]{1,0:T(4,128)(2,1)}, u32[]{:S(2)}) copy-start(bf16[3,512]{1,0:T(4,128)(2,1)} %lq_ref.1) | copy-start | bytes 9220
  0.9 44.8 %copy-start.6 = (f32[2,512]{1,0:T(2,128)S(1)}, f32[2,512]{1,0:T(2,128)}, u32[]{:S(2)}) copy-start(f32[2,512]{1,0:T(2,128)} %gains_ref.1) | copy-start | bytes 12292

commit v6 on v5

--- a/solution.py
+++ b/solution.py
@@ -191,22 +191,24 @@
         for n, score in enumerate(scores):
             weight = jnp.exp(score - top)
             total = total + weight
-            p_scr[half, n * BOTH : (n + 1) * BOTH, :] = jnp.where(lane_wide < STATS // 2, weight, 0.0).astype(BF16)
+            p_scr[half, n * BOTH : (n + 1) * BOTH, :] = weight.astype(BF16).astype(F32)
         stats = jnp.where(lane_wide < STATS // 2, top, pltpu.roll(total, STATS // 2, 1))
         kstat[index, 0:PATCHES, :] = stats[:PATCHES]
         sstat[index, 0:PATCHES, :] = stats[PATCHES:]
-        for at in range(0, LATENT * D, 256):
-            wide = dot(p_scr[half], ex_scr[:, at : at + 256])
-            for side in range(2):
-                lanes = (at % D) // 128 + side
-                here = sum(
-                    v_scr[index, lanes, member, :]
-                    * wide[n * BOTH : (n + 1) * BOTH, side * 128 : (side + 1) * 128]
-                    for n, member in enumerate(members)
-                )
-                columns = slice(at + side * 128, at + (side + 1) * 128)
-                keep[index, 0:PATCHES, columns] = here[:PATCHES]
-                snum[index, 0:PATCHES, columns] = here[PATCHES:].astype(BF16)
+        for lanes in range(D // 128):
+            sums = [jnp.zeros((BOTH, 128), F32) for _ in range(LATENT)]
+            for n, member in enumerate(members):
+                value = v_scr[index, lanes, member, :]
+                weight = p_scr[half, n * BOTH : (n + 1) * BOTH, :]
+                for j in range(LATENT):
+                    column = (lane_wide >> 5) + (j * HEADS + lanes * 4)
+                    sums[j] += value * jnp.take_along_axis(
+                        weight, column, axis=1, mode="promise_in_bounds"
+                    )
+            for j in range(LATENT):
+                columns = slice(j * D + lanes * 128, j * D + (lanes + 1) * 128)
+                keep[index, 0:PATCHES, columns] = sums[j][:PATCHES]
+                snum[index, 0:PATCHES, columns] = sums[j][PATCHES:].astype(BF16)
         _, second = partners(half, slot)
         for src, dst, send, recv in (
             (snum, rnum, num_send, num_recv), (sstat, rstat, stat_send, stat_recv)
@@ -404,7 +406,7 @@
             pltpu.VMEM((STATS, LATENT * D), BF16),
             pltpu.VMEM((pieces, GATHERED, STATS), F32),
             pltpu.VMEM((pieces, D // 128, GATHERED, 128), F32),
-            pltpu.VMEM((2, GATHERED, STATS), BF16),
+            pltpu.VMEM((2, GATHERED, STATS), F32),
             pltpu.VMEM((RING * PAD, LATENT * D), F32),
             pltpu.VMEM((RING * PAD, STATS), F32),
             pltpu.VMEM((pieces, PAD, LATENT * D), F32),

time: 53.7 us -> 53.9 us (level)
  no operation moved by 1% of the time
where the time goes in v6:
time: 53.9 us; the launch traced here: 53.8 us
  Pallas kernels  52.7 us (98%)
  local copies, waits for them, and re-layouts  0.85 us (2%)
    pallas_call x1, Pallas kernels, body(): pl.pallas_call(gather_kernel, out_shape=jax.ShapeDtypeStruct((ROWS, D), B...  44.9 us
    pallas_call x1, Pallas kernels, body(): pl.pallas_call(window_kernel, out_shape=jax.ShapeDtypeStruct((WLAT, 2 * H...  7.77 us

profile of v6, /device:TPU:1, one launch (start us, length us, event | category | flops | bytes accessed | tf_op | source)
XLA Modules:
  0.0 53.8 jit_solution(15654619293538080804)
XLA Ops:
  0.0 0.0 copy-start.1
  0.0 0.0 copy-start
  0.0 0.0 copy-start.4
  0.0 0.0 copy-start.2
  0.0 0.0 copy-start.3
  0.0 0.0 copy-start.5
  0.0 0.8 %copy-done.5 = bf16[3,512]{1,0:T(4,128)(2,1)S(1)} copy-done((bf16[3,512]{1,0:T(4,128)(2,1)S(1)}, bf16[3,512]{1,0:T(4,128)(2,1)}, u32[]{:S(2)}) %copy-start.5) | copy-done | bytes 3096
  0.9 0.0 copy-start.6
  0.9 44.9 %shard_map.118.latent_ref = bf16[240,512]{1,0:T(8,128)(2,1)S(1)} custom-call(bf16[96,12,4,512]{3,2,1,0:T(4,128)(2,1)} %tokens.1, bf16[512,512]{1,0:T(8,128)(2,1)} %w_pq.1, bf16[512,512]{1,0:T(8,128)(2,1)} %w_pk.1, bf16[512,512]{1,0:T(8,128)(2,1)} %w_pv.1, bf16[512,512]{1,0:T(8,128)(2,1)} %w_po.1, bf16[3,512]{1,0:T(4,128)(2,1)S(1)} %copy-done.5), custom_call_target="tpu_custom_call" | custom-call | flops 8000000000 | bytes 100000000 | tf_op jit(solution)/shard_map/pallas_call | solution.py:397
  45.8 0.0 copy-done.1
  45.8 0.0 copy-done
  45.8 0.0 copy-done.4
  45.8 0.0 copy-done.2
  45.8 0.0 copy-done.3
  45.8 0.0 copy-done.6
  45.8 7.8 %shard_map.119 = bf16[6,12,3,512]{3,2,1,0:T(4,128)(2,1)} custom-call(bf16[240,512]{1,0:T(8,128)(2,1)S(1)} %shard_map.118.latent_ref, f32[2,512]{1,0:T(2,128)S(1)} %copy-done.6, bf16[512,512]{1,0:T(8,128)(2,1)S(1)} %copy-done.3, bf16[512,1024]{1,0:T(8,128)(2,1)S(1)} %copy-done.2, bf16[512,512]{1,0:T(8,128)(2,1)S(1)} %copy-done.4, ...), custom_call_target="tpu_custom_call" | custom-call | flops 2000000000 | bytes 7000000 | tf_op jit(solution)/shard_map/pallas_call | solution.py:444
Async XLA Ops:
  0.0 45.8 %copy-start.1 = (bf16[2048,512]{1,0:T(8,128)(2,1)S(1)}, bf16[2048,512]{1,0:T(8,128)(2,1)}, u32[]{:S(2)}) copy-start(bf16[2048,512]{1,0:T(8,128)(2,1)} %w_down.1) | copy-start | bytes 6291460
  0.0 45.8 %copy-start = (bf16[512,2048]{1,0:T(8,128)(2,1)S(1)}, bf16[512,2048]{1,0:T(8,128)(2,1)}, u32[]{:S(2)}) copy-start(bf16[512,2048]{1,0:T(8,128)(2,1)} %w_up.1) | copy-start | bytes 6291460
  0.0 45.8 %copy-start.4 = (bf16[512,512]{1,0:T(8,128)(2,1)S(1)}, bf16[512,512]{1,0:T(8,128)(2,1)}, u32[]{:S(2)}) copy-start(bf16[512,512]{1,0:T(8,128)(2,1)} %w_so.1) | copy-start | bytes 1572868
  0.0 45.8 %copy-start.2 = (bf16[512,1024]{1,0:T(8,128)(2,1)S(1)}, bf16[512,1024]{1,0:T(8,128)(2,1)}, u32[]{:S(2)}) copy-start(bf16[512,1024]{1,0:T(8,128)(2,1)} %w_skv.1) | copy-start | bytes 3145732
  0.0 45.8 %copy-start.3 = (bf16[512,512]{1,0:T(8,128)(2,1)S(1)}, bf16[512,512]{1,0:T(8,128)(2,1)}, u32[]{:S(2)}) copy-start(bf16[512,512]{1,0:T(8,128)(2,1)} %w_sq.1) | copy-start | bytes 1572868
  0.0 0.8 %copy-start.5 = (bf16[3,512]{1,0:T(4,128)(2,1)S(1)}, bf16[3,512]{1,0:T(4,128)(2,1)}, u32[]{:S(2)}) copy-start(bf16[3,512]{1,0:T(4,128)(2,1)} %lq_ref.1) | copy-start | bytes 9220
  0.9 45.0 %copy-start.6 = (f32[2,512]{1,0:T(2,128)S(1)}, f32[2,512]{1,0:T(2,128)}, u32[]{:S(2)}) copy-start(f32[2,512]{1,0:T(2,128)} %gains_ref.1) | copy-start | bytes 12292

commit v7 on v5

--- a/solution.py
+++ b/solution.py
@@ -255,13 +255,23 @@
                     device_id_type=MESH,
                 ).start()
 
-    for half, k in order:
-        own = buf.at[half, slot_of(half, k), 0]
-        pltpu.make_async_copy(own, own, own_sem.at[half, slot_of(half, k)]).wait()
+    def own_products(half, k):
+        slot = slot_of(half, k)
+        own = buf.at[half, slot, 0]
+        pltpu.make_async_copy(own, own, own_sem.at[half, slot]).wait()
         products(half, k, 0)
+
+    for half, k in order[:4]:
+        own_products(half, k)
+    for k in range(2):
+        for half in (1, 0):
+            arrive(half, k)
+        for half in (1, 0):
+            own_products(half, k + 2)
     for k in range(RING):
         for half in (1, 0):
-            arrive(half, k)
+            if k >= 2:
+                arrive(half, k)
         for half in (1, 0):
             products(half, k, 1)
         for half in (1, 0):

time: 53.7 us -> 57.3 us (1.067); the launches traced: 53.6 us -> 56.3 us
  Pallas kernels: 52.5 us -> 55.2 us
    pallas_call x1, Pallas kernels: 44.7 us -> 47.4 us  [body(): pl.pallas_call(gather_kernel, out_shape=jax.ShapeDtypeStruct((ROWS, D), B...]
where the time goes in v7:
time: 57.3 us; the launch traced here: 56.3 us
  Pallas kernels  55.2 us (96%)
  local copies, waits for them, and re-layouts  0.85 us (1%)
    pallas_call x1, Pallas kernels, body(): pl.pallas_call(gather_kernel, out_shape=jax.ShapeDtypeStruct((ROWS, D), B...  47.4 us
    pallas_call x1, Pallas kernels, body(): pl.pallas_call(window_kernel, out_shape=jax.ShapeDtypeStruct((WLAT, 2 * H...  7.77 us

profile of v7, /device:TPU:1, one launch (start us, length us, event | category | flops | bytes accessed | tf_op | source)
XLA Modules:
  0.0 56.3 jit_solution(13844108535365594276)
XLA Ops:
  0.0 0.0 copy-start.1
  0.0 0.0 copy-start
  0.0 0.0 copy-start.4
  0.0 0.0 copy-start.2
  0.0 0.0 copy-start.3
  0.0 0.0 copy-start.5
  0.0 0.8 %copy-done.5 = bf16[3,512]{1,0:T(4,128)(2,1)S(1)} copy-done((bf16[3,512]{1,0:T(4,128)(2,1)S(1)}, bf16[3,512]{1,0:T(4,128)(2,1)}, u32[]{:S(2)}) %copy-start.5) | copy-done | bytes 3096
  0.9 0.0 copy-start.6
  0.9 47.4 %shard_map.118.latent_ref = bf16[240,512]{1,0:T(8,128)(2,1)S(1)} custom-call(bf16[96,12,4,512]{3,2,1,0:T(4,128)(2,1)} %tokens.1, bf16[512,512]{1,0:T(8,128)(2,1)} %w_pq.1, bf16[512,512]{1,0:T(8,128)(2,1)} %w_pk.1, bf16[512,512]{1,0:T(8,128)(2,1)} %w_pv.1, bf16[512,512]{1,0:T(8,128)(2,1)} %w_po.1, bf16[3,512]{1,0:T(4,128)(2,1)S(1)} %copy-done.5), custom_call_target="tpu_custom_call" | custom-call | flops 8000000000 | bytes 100000000 | tf_op jit(solution)/shard_map/pallas_call | solution.py:405
  48.3 0.0 copy-done.1
  48.3 0.0 copy-done
  48.3 0.0 copy-done.4
  48.3 0.0 copy-done.2
  48.3 0.0 copy-done.3
  48.3 0.0 copy-done.6
  48.3 7.8 %shard_map.119 = bf16[6,12,3,512]{3,2,1,0:T(4,128)(2,1)} custom-call(bf16[240,512]{1,0:T(8,128)(2,1)S(1)} %shard_map.118.latent_ref, f32[2,512]{1,0:T(2,128)S(1)} %copy-done.6, bf16[512,512]{1,0:T(8,128)(2,1)S(1)} %copy-done.3, bf16[512,1024]{1,0:T(8,128)(2,1)S(1)} %copy-done.2, bf16[512,512]{1,0:T(8,128)(2,1)S(1)} %copy-done.4, ...), custom_call_target="tpu_custom_call" | custom-call | flops 2000000000 | bytes 7000000 | tf_op jit(solution)/shard_map/pallas_call | solution.py:452
Async XLA Ops:
  0.0 48.3 %copy-start.1 = (bf16[2048,512]{1,0:T(8,128)(2,1)S(1)}, bf16[2048,512]{1,0:T(8,128)(2,1)}, u32[]{:S(2)}) copy-start(bf16[2048,512]{1,0:T(8,128)(2,1)} %w_down.1) | copy-start | bytes 6291460
  0.0 48.3 %copy-start = (bf16[512,2048]{1,0:T(8,128)(2,1)S(1)}, bf16[512,2048]{1,0:T(8,128)(2,1)}, u32[]{:S(2)}) copy-start(bf16[512,2048]{1,0:T(8,128)(2,1)} %w_up.1) | copy-start | bytes 6291460
  0.0 48.3 %copy-start.4 = (bf16[512,512]{1,0:T(8,128)(2,1)S(1)}, bf16[512,512]{1,0:T(8,128)(2,1)}, u32[]{:S(2)}) copy-start(bf16[512,512]{1,0:T(8,128)(2,1)} %w_so.1) | copy-start | bytes 1572868
  0.0 48.3 %copy-start.2 = (bf16[512,1024]{1,0:T(8,128)(2,1)S(1)}, bf16[512,1024]{1,0:T(8,128)(2,1)}, u32[]{:S(2)}) copy-start(bf16[512,1024]{1,0:T(8,128)(2,1)} %w_skv.1) | copy-start | bytes 3145732
  0.0 48.3 %copy-start.3 = (bf16[512,512]{1,0:T(8,128)(2,1)S(1)}, bf16[512,512]{1,0:T(8,128)(2,1)}, u32[]{:S(2)}) copy-start(bf16[512,512]{1,0:T(8,128)(2,1)} %w_sq.1) | copy-start | bytes 1572868
  0.0 0.8 %copy-start.5 = (bf16[3,512]{1,0:T(4,128)(2,1)S(1)}, bf16[3,512]{1,0:T(4,128)(2,1)}, u32[]{:S(2)}) copy-start(bf16[3,512]{1,0:T(4,128)(2,1)} %lq_ref.1) | copy-start | bytes 9220
  0.9 47.5 %copy-start.6 = (f32[2,512]{1,0:T(2,128)S(1)}, f32[2,512]{1,0:T(2,128)}, u32[]{:S(2)}) copy-start(f32[2,512]{1,0:T(2,128)} %gains_ref.1) | copy-start | bytes 12292

commit v8 on v5

--- a/solution.py
+++ b/solution.py
@@ -27,6 +27,9 @@
 PAD = 40
 ROWS = 2 * LATENT * PAD
 STATS = 128
+FULL = 32
+WIDTH = LATENT * D + 256
+FOLD = 24
 MESH = pl.DeviceIdType.MESH
 epsilon = 1e-05
 
@@ -59,7 +62,7 @@
     tokens, w_pq, w_pk, w_pv, w_po, lq_ref,
     out_ref,
     buf, pq, pk, pv, po,
-    kp_scr, ex_scr, s_scr, v_scr, p_scr, px_scr, sc_scr, keep, kstat, snum, rnum, sstat, rstat,
+    kp_scr, ex_scr, s_scr, v_scr, p_scr, px_scr, sc_scr, keep, kstat, t_scr, snum, rnum, sstat, rstat,
     fnum, gnum, fstat, gstat, att_scr,
     w_sem, own_sem, tok_send, tok_recv, num_send, num_recv, stat_send, stat_recv,
     far_send, far_recv, fst_send, fst_recv,
@@ -159,6 +162,27 @@
         low = lax.broadcasted_iota(jnp.int32, scales.shape, 1) < STATS // 2
         return dot(jnp.where(low, head, rest).astype(BF16), ex_scr[...])
 
+    def fold(stats):
+        low = lax.broadcasted_iota(jnp.int32, (PAD - FOLD, STATS), 1) < STATS // 2
+        rest = pltpu.roll(stats[FOLD:PAD], STATS // 2, 1)
+        return jnp.concatenate(
+            [jnp.where(low, stats[: PAD - FOLD], rest), stats[PAD - FOLD : FOLD]], axis=0
+        )
+
+    def unfold(stats):
+        return jnp.concatenate([stats, pltpu.roll(stats[: PAD - FOLD], STATS // 2, 1)], axis=0)
+
+    def pack(ref, at, group, rows):
+        rows = rows.astype(BF16)
+        ref[at, 0:FULL, group * 256 : (group + 1) * 256] = rows[:FULL]
+        ref[at, group * 4 : group * 4 + 4, LATENT * D :] = rows[FULL:PATCHES]
+
+    def unpack(rows, group):
+        rest = rows[:, LATENT * D :].astype(F32)[group * 4 : group * 4 + 4]
+        return jnp.concatenate(
+            [rows[:, group * 256 : (group + 1) * 256].astype(F32), rest], axis=0
+        )
+
     lane_wide = lax.broadcasted_iota(jnp.int32, (BOTH, STATS), 1)
 
     def products(half, k, src):
@@ -187,26 +211,28 @@
         ]
         scores = [s_scr[index, member, :] for member in members]
         top = functools.reduce(jnp.maximum, scores)
-        total = jnp.zeros_like(top)
-        for n, score in enumerate(scores):
-            weight = jnp.exp(score - top)
-            total = total + weight
-            p_scr[half, n * BOTH : (n + 1) * BOTH, :] = jnp.where(lane_wide < STATS // 2, weight, 0.0).astype(BF16)
-        stats = jnp.where(lane_wide < STATS // 2, top, pltpu.roll(total, STATS // 2, 1))
+        weights = [jnp.exp(score - top) for score in scores]
+        total = sum(weights)
+        inverse = jnp.where(lane_wide < STATS // 2, 1.0 / total, 0.0)
+        for n, weight in enumerate(weights):
+            p_scr[half, n * BOTH : (n + 1) * BOTH, :] = (weight * inverse).astype(BF16)
+        stats = top + jnp.log(total)
         kstat[index, 0:PATCHES, :] = stats[:PATCHES]
-        sstat[index, 0:PATCHES, :] = stats[PATCHES:]
+        t_scr[half, 0:PATCHES, :] = stats[PATCHES:]
+        sstat[index] = fold(t_scr[half])
         for at in range(0, LATENT * D, 256):
             wide = dot(p_scr[half], ex_scr[:, at : at + 256])
-            for side in range(2):
-                lanes = (at % D) // 128 + side
-                here = sum(
-                    v_scr[index, lanes, member, :]
+            sides = [
+                sum(
+                    v_scr[index, (at % D) // 128 + side, member, :]
                     * wide[n * BOTH : (n + 1) * BOTH, side * 128 : (side + 1) * 128]
                     for n, member in enumerate(members)
                 )
-                columns = slice(at + side * 128, at + (side + 1) * 128)
-                keep[index, 0:PATCHES, columns] = here[:PATCHES]
-                snum[index, 0:PATCHES, columns] = here[PATCHES:].astype(BF16)
+                for side in range(2)
+            ]
+            here = jnp.concatenate(sides, axis=1)
+            keep[index, 0:PATCHES, at : at + 256] = here[:PATCHES]
+            pack(snum, index, at // 256, here[PATCHES:])
         _, second = partners(half, slot)
         for src, dst, send, recv in (
             (snum, rnum, num_send, num_recv), (sstat, rstat, stat_send, stat_recv)
@@ -224,20 +250,21 @@
         slot = slot_of(half, k)
         index = half * RING + k
         pltpu.make_async_copy(rstat.at[index], rstat.at[index], stat_recv.at[index]).wait()
-        mine, theirs = kstat[index], rstat[index]
+        mine, theirs = kstat[index], unfold(rstat[index])
         top = jnp.maximum(mine, theirs)
         my_scale, their_scale = jnp.exp(mine - top), jnp.exp(theirs - top)
-        total = (
-            pltpu.roll(mine, STATS // 2, 1) * my_scale
-            + pltpu.roll(theirs, STATS // 2, 1) * their_scale
-        )
-        fstat[index] = jnp.where(lane < STATS // 2, top, pltpu.roll(total, STATS // 2, 1))
-        scales = jnp.concatenate([my_scale, their_scale], axis=0)
-        scales = widen(scales)
+        total = my_scale + their_scale
+        fstat[index] = fold(top + jnp.log(total))
+        scales = widen(jnp.concatenate([my_scale / total, their_scale / total], axis=0))
         pltpu.make_async_copy(rnum.at[index], rnum.at[index], num_recv.at[index]).wait()
-        fnum[index] = (
-            keep[index] * scales[:PAD] + rnum[index].astype(F32) * scales[PAD:]
-        ).astype(BF16)
+        theirs = rnum[index]
+        for group in range(LATENT * D // 256):
+            columns = slice(group * 256, (group + 1) * 256)
+            merged = (
+                keep[index, 0:PATCHES, columns] * scales[0:PATCHES, columns]
+                + unpack(theirs, group) * scales[PAD : PAD + PATCHES, columns]
+            )
+            pack(fnum, index, group, merged)
         source = y if half == 0 else x
         there = slot * RING + x if half == 0 else y * RING + slot
         for src, dst, send, recv in (
@@ -271,29 +298,28 @@
     for half in (1, 0):
         merge(half, RING - 1)
 
+    att_scr[...] = jnp.zeros_like(att_scr)
     inside = lax.broadcasted_iota(jnp.int32, (PAD, STATS), 0) < PATCHES
     for half in range(2):
         pltpu.make_async_copy(gnum.at[half], gnum.at[half], far_recv.at[half]).wait()
         pltpu.make_async_copy(gstat.at[half], gstat.at[half], fst_recv.at[half]).wait()
-        stats = [gstat[half, src] for src in range(RING)]
+        stats = [unfold(gstat[half, src]) for src in range(RING)]
         top = functools.reduce(jnp.maximum, stats)
         scales = [jnp.exp(stat - top) for stat in stats]
-        denominator = sum(
-            pltpu.roll(stat, STATS // 2, 1) * scale for stat, scale in zip(stats, scales)
-        )
+        denominator = sum(scales)
         valid = (lane < LATENT * HEADS) & inside
         for src in range(RING):
             sc_scr[pl.ds(src * PAD, PAD), :] = jnp.where(valid, scales[src] / denominator, 0.0)
         px_scr[0 : RING * PAD] = widen(sc_scr[...])
-        inside_wide = lax.broadcasted_iota(jnp.int32, (PAD, D), 0) < PATCHES
-        for j in range(LATENT):
+        gathered = [gnum[half, src] for src in range(RING)]
+        for group in range(LATENT * D // 256):
             share = sum(
-                gnum[half, src, :, j * D : (j + 1) * D].astype(F32)
-                * px_scr[pl.ds(src * PAD, PAD), j * D : (j + 1) * D]
+                unpack(gathered[src], group)
+                * px_scr[pl.ds(src * PAD, PATCHES), group * 256 : (group + 1) * 256]
                 for src in range(RING)
             )
-            att_scr[pl.ds((half * LATENT + j) * PAD, PAD), :] = jnp.where(inside_wide, share, 0.0)
-
+            at = (half * LATENT + group // 2) * PAD
+            att_scr[at : at + PATCHES, group % 2 * 256 : (group % 2 + 1) * 256] = share
     loads[3].wait()
     latent = dot(att_scr[...].astype(BF16), po[...])
     start = jnp.concatenate(
@@ -409,14 +435,15 @@
             pltpu.VMEM((RING * PAD, STATS), F32),
             pltpu.VMEM((pieces, PAD, LATENT * D), F32),
             pltpu.VMEM((pieces, PAD, STATS), F32),
-            pltpu.VMEM((pieces, PAD, LATENT * D), BF16),
-            pltpu.VMEM((pieces, PAD, LATENT * D), BF16),
-            pltpu.VMEM((pieces, PAD, STATS), F32),
-            pltpu.VMEM((pieces, PAD, STATS), F32),
-            pltpu.VMEM((pieces, PAD, LATENT * D), BF16),
-            pltpu.VMEM((2, RING, PAD, LATENT * D), BF16),
-            pltpu.VMEM((pieces, PAD, STATS), F32),
-            pltpu.VMEM((2, RING, PAD, STATS), F32),
+            pltpu.VMEM((2, PAD, STATS), F32),
+            pltpu.VMEM((pieces, FULL, WIDTH), BF16),
+            pltpu.VMEM((pieces, FULL, WIDTH), BF16),
+            pltpu.VMEM((pieces, FOLD, STATS), F32),
+            pltpu.VMEM((pieces, FOLD, STATS), F32),
+            pltpu.VMEM((pieces, FULL, WIDTH), BF16),
+            pltpu.VMEM((2, RING, FULL, WIDTH), BF16),
+            pltpu.VMEM((pieces, FOLD, STATS), F32),
+            pltpu.VMEM((2, RING, FOLD, STATS), F32),
             pltpu.VMEM((ROWS, D), F32),
             pltpu.SemaphoreType.DMA((len(matrices),)),
             pltpu.SemaphoreType.DMA((2, RING)),

time: 53.7 us -> 51.9 us (0.966)
  Pallas kernels: 52.5 us -> 50.7 us
    pallas_call x1, Pallas kernels: 44.7 us -> 42.9 us  [body(): pl.pallas_call(gather_kernel, out_shape=jax.ShapeDtypeStruct((ROWS, D), B...]
where the time goes in v8:
time: 51.9 us; the launch traced here: 51.8 us
  Pallas kernels  50.7 us (98%)
  local copies, waits for them, and re-layouts  0.85 us (2%)
    pallas_call x1, Pallas kernels, body(): pl.pallas_call(gather_kernel, out_shape=jax.ShapeDtypeStruct((ROWS, D), B...  42.9 us
    pallas_call x1, Pallas kernels, body(): pl.pallas_call(window_kernel, out_shape=jax.ShapeDtypeStruct((WLAT, 2 * H...  7.78 us

profile of v8, /device:TPU:1, one launch (start us, length us, event | category | flops | bytes accessed | tf_op | source)
XLA Modules:
  0.0 51.8 jit_solution(18238372461446004470)
XLA Ops:
  0.0 0.0 copy-start.1
  0.0 0.0 copy-start
  0.0 0.0 copy-start.4
  0.0 0.0 copy-start.2
  0.0 0.0 copy-start.3
  0.0 0.0 copy-start.5
  0.0 0.8 %copy-done.5 = bf16[3,512]{1,0:T(4,128)(2,1)S(1)} copy-done((bf16[3,512]{1,0:T(4,128)(2,1)S(1)}, bf16[3,512]{1,0:T(4,128)(2,1)}, u32[]{:S(2)}) %copy-start.5) | copy-done | bytes 3096
  0.9 0.0 copy-start.6
  0.9 42.9 %shard_map.118.latent_ref = bf16[240,512]{1,0:T(8,128)(2,1)S(1)} custom-call(bf16[96,12,4,512]{3,2,1,0:T(4,128)(2,1)} %tokens.1, bf16[512,512]{1,0:T(8,128)(2,1)} %w_pq.1, bf16[512,512]{1,0:T(8,128)(2,1)} %w_pk.1, bf16[512,512]{1,0:T(8,128)(2,1)} %w_pv.1, bf16[512,512]{1,0:T(8,128)(2,1)} %w_po.1, bf16[3,512]{1,0:T(4,128)(2,1)S(1)} %copy-done.5), custom_call_target="tpu_custom_call" | custom-call | flops 8000000000 | bytes 100000000 | tf_op jit(solution)/shard_map/pallas_call | solution.py:421
  43.8 0.0 copy-done.1
  43.8 0.0 copy-done
  43.8 0.0 copy-done.4
  43.8 0.0 copy-done.2
  43.8 0.0 copy-done.3
  43.8 0.0 copy-done.6
  43.8 7.8 %shard_map.119 = bf16[6,12,3,512]{3,2,1,0:T(4,128)(2,1)} custom-call(bf16[240,512]{1,0:T(8,128)(2,1)S(1)} %shard_map.118.latent_ref, f32[2,512]{1,0:T(2,128)S(1)} %copy-done.6, bf16[512,512]{1,0:T(8,128)(2,1)S(1)} %copy-done.3, bf16[512,1024]{1,0:T(8,128)(2,1)S(1)} %copy-done.2, bf16[512,512]{1,0:T(8,128)(2,1)S(1)} %copy-done.4, ...), custom_call_target="tpu_custom_call" | custom-call | flops 2000000000 | bytes 7000000 | tf_op jit(solution)/shard_map/pallas_call | solution.py:469
Async XLA Ops:
  0.0 43.8 %copy-start.1 = (bf16[2048,512]{1,0:T(8,128)(2,1)S(1)}, bf16[2048,512]{1,0:T(8,128)(2,1)}, u32[]{:S(2)}) copy-start(bf16[2048,512]{1,0:T(8,128)(2,1)} %w_down.1) | copy-start | bytes 6291460
  0.0 43.8 %copy-start = (bf16[512,2048]{1,0:T(8,128)(2,1)S(1)}, bf16[512,2048]{1,0:T(8,128)(2,1)}, u32[]{:S(2)}) copy-start(bf16[512,2048]{1,0:T(8,128)(2,1)} %w_up.1) | copy-start | bytes 6291460
  0.0 43.8 %copy-start.4 = (bf16[512,512]{1,0:T(8,128)(2,1)S(1)}, bf16[512,512]{1,0:T(8,128)(2,1)}, u32[]{:S(2)}) copy-start(bf16[512,512]{1,0:T(8,128)(2,1)} %w_so.1) | copy-start | bytes 1572868
  0.0 43.8 %copy-start.2 = (bf16[512,1024]{1,0:T(8,128)(2,1)S(1)}, bf16[512,1024]{1,0:T(8,128)(2,1)}, u32[]{:S(2)}) copy-start(bf16[512,1024]{1,0:T(8,128)(2,1)} %w_skv.1) | copy-start | bytes 3145732
  0.0 43.8 %copy-start.3 = (bf16[512,512]{1,0:T(8,128)(2,1)S(1)}, bf16[512,512]{1,0:T(8,128)(2,1)}, u32[]{:S(2)}) copy-start(bf16[512,512]{1,0:T(8,128)(2,1)} %w_sq.1) | copy-start | bytes 1572868
  0.0 0.8 %copy-start.5 = (bf16[3,512]{1,0:T(4,128)(2,1)S(1)}, bf16[3,512]{1,0:T(4,128)(2,1)}, u32[]{:S(2)}) copy-start(bf16[3,512]{1,0:T(4,128)(2,1)} %lq_ref.1) | copy-start | bytes 9220
  0.9 43.0 %copy-start.6 = (f32[2,512]{1,0:T(2,128)S(1)}, f32[2,512]{1,0:T(2,128)}, u32[]{:S(2)}) copy-start(f32[2,512]{1,0:T(2,128)} %gains_ref.1) | copy-start | bytes 12292

commit v9 on v8

--- a/solution.py
+++ b/solution.py
@@ -25,7 +25,7 @@
 BOTH = 2 * PATCHES
 GATHERED = 2 * BOTH * LEVS
 PAD = 40
-ROWS = 2 * LATENT * PAD
+ROWS = 2 * LATENT * PATCHES
 STATS = 128
 FULL = 32
 WIDTH = LATENT * D + 256
@@ -61,7 +61,7 @@
 def gather_kernel(
     tokens, w_pq, w_pk, w_pv, w_po, lq_ref,
     out_ref,
-    buf, pq, pk, pv, po,
+    buf, pq, pk, pv, po, lq_scr,
     kp_scr, ex_scr, s_scr, v_scr, p_scr, px_scr, sc_scr, keep, kstat, t_scr, snum, rnum, sstat, rstat,
     fnum, gnum, fstat, gstat, att_scr,
     w_sem, own_sem, tok_send, tok_recv, num_send, num_recv, stat_send, stat_recv,
@@ -124,7 +124,7 @@
                         device_id_type=MESH,
                     ).start()
 
-    weights = ((w_pq, pq), (w_pk, pk), (w_pv, pv), (w_po, po))
+    weights = ((w_pq, pq), (w_pk, pk), (w_pv, pv), (w_po, po), (lq_ref, lq_scr))
     loads = [pltpu.make_async_copy(src, dst, w_sem.at[i]) for i, (src, dst) in enumerate(weights)]
     for load in loads:
         load.start()
@@ -141,7 +141,8 @@
         (row & (STATS // 2 - 1)) == (col >> 9) * HEADS + ((col & (D - 1)) >> 5), 1.0, 0.0
     ).astype(BF16)
     loads[0].wait()
-    queries = dot(lq_ref[...], pq[...])
+    loads[4].wait()
+    queries = dot(lq_scr[...], pq[...])
     head_row = lax.broadcasted_iota(jnp.int32, (HEADS, D), 0)
     head_col = lax.broadcasted_iota(jnp.int32, (HEADS, D), 1) >> 5
     spread = jnp.concatenate(
@@ -298,7 +299,6 @@
     for half in (1, 0):
         merge(half, RING - 1)
 
-    att_scr[...] = jnp.zeros_like(att_scr)
     inside = lax.broadcasted_iota(jnp.int32, (PAD, STATS), 0) < PATCHES
     for half in range(2):
         pltpu.make_async_copy(gnum.at[half], gnum.at[half], far_recv.at[half]).wait()
@@ -318,18 +318,16 @@
                 * px_scr[pl.ds(src * PAD, PATCHES), group * 256 : (group + 1) * 256]
                 for src in range(RING)
             )
-            at = (half * LATENT + group // 2) * PAD
+            at = (half * LATENT + group // 2) * PATCHES
             att_scr[at : at + PATCHES, group % 2 * 256 : (group % 2 + 1) * 256] = share
     loads[3].wait()
     latent = dot(att_scr[...].astype(BF16), po[...])
-    start = jnp.concatenate(
-        [
-            jnp.broadcast_to(lq_ref[j : j + 1, :].astype(F32), (PAD, D))
-            for _ in range(2)
-            for j in range(LATENT)
-        ],
-        axis=0,
-    )
+    token = lax.broadcasted_iota(jnp.int32, (ROWS, D), 0)
+    block = sum((token >= b * PATCHES).astype(jnp.int32) for b in range(1, 2 * LATENT))
+    level = jnp.where(block >= LATENT, block - LATENT, block)
+    start = jnp.zeros((ROWS, D), F32)
+    for j in range(LATENT):
+        start = jnp.where(level == j, lq_scr[j : j + 1, :].astype(F32), start)
     out_ref[...] = (start + latent).astype(BF16)
 
     for half in range(2):
@@ -363,18 +361,14 @@
     keys = keyvals[:, :D]
     vt_scr[...] = jnp.transpose(keyvals[:, D:]).astype(BF16)
 
-    def place(shape, axis):
+    def southern(shape, axis):
         index = lax.broadcasted_iota(jnp.int32, shape, axis)
         for b in range(2 * LATENT - 1, 0, -1):
-            index = jnp.where(index >= b * PAD, index - b * PAD, index)
-        return index
-
-    key_at = place((ROWS, ROWS), 0)
-    query_at = place((ROWS, ROWS), 1)
-    cut = WLAT // 2 * HALF
-    apart = (key_at >= cut) != (query_at >= cut)
-    excluded = (key_at >= PATCHES) | (apart & (var == N_VAR - 1))
-    bias = jnp.where(excluded, -jnp.inf, 0.0)
+            index = jnp.where(index >= b * PATCHES, index - b * PATCHES, index)
+        return index >= WLAT // 2 * HALF
+
+    apart = southern((ROWS, ROWS), 0) != southern((ROWS, ROWS), 1)
+    bias = jnp.where(apart & (var == N_VAR - 1), -jnp.inf, 0.0)
     lane_head = lax.broadcasted_iota(jnp.int32, (ROWS, 256), 1) >> 5
     for h in range(HEADS):
         at = h // 8 * 256
@@ -400,7 +394,7 @@
         half, j = b // LATENT, b % LATENT
         for l in range(lanes):
             turn_scr[l, pl.ds(half * PATCHES * 4 + j, PATCHES, stride=4), :] = residual[
-                b * PAD : b * PAD + PATCHES, l * 128 : (l + 1) * 128
+                b * PATCHES : (b + 1) * PATCHES, l * 128 : (l + 1) * 128
             ]
     for half in range(2):
         for r in range(WLAT):
@@ -421,11 +415,11 @@
     latent = pl.pallas_call(
         gather_kernel,
         out_shape=jax.ShapeDtypeStruct((ROWS, D), BF16),
-        in_specs=[whole] * (1 + len(matrices)) + [near],
+        in_specs=[whole] * (2 + len(matrices)),
         out_specs=near,
         scratch_shapes=[
             pltpu.VMEM((2, RING, 2, 2, WLAT, HALF, LEVS, D), BF16),
-            *[pltpu.VMEM(m.shape, m.dtype) for m in matrices],
+            *[pltpu.VMEM(m.shape, m.dtype) for m in (*matrices, latent_queries)],
             pltpu.VMEM((STATS, D), BF16),
             pltpu.VMEM((STATS, LATENT * D), BF16),
             pltpu.VMEM((pieces, GATHERED, STATS), F32),
@@ -445,7 +439,7 @@
             pltpu.VMEM((pieces, FOLD, STATS), F32),
             pltpu.VMEM((2, RING, FOLD, STATS), F32),
             pltpu.VMEM((ROWS, D), F32),
-            pltpu.SemaphoreType.DMA((len(matrices),)),
+            pltpu.SemaphoreType.DMA((1 + len(matrices),)),
             pltpu.SemaphoreType.DMA((2, RING)),
             pltpu.SemaphoreType.DMA((2, RING)),
             pltpu.SemaphoreType.DMA((2, RING)),

time: 51.9 us -> 51.6 us (level)
  no operation moved by 1% of the time
where the time goes in v9:
time: 51.6 us; the launch traced here: 51.5 us
  Pallas kernels  50.4 us (98%)
  local copies, waits for them, and re-layouts  0.85 us (2%)
    pallas_call x1, Pallas kernels, body(): pl.pallas_call(gather_kernel, out_shape=jax.ShapeDtypeStruct((ROWS, D), B...  42.9 us
    pallas_call x1, Pallas kernels, body(): pl.pallas_call(window_kernel, out_shape=jax.ShapeDtypeStruct((WLAT, 2 * H...  7.51 us

profile of v9, /device:TPU:1, one launch (start us, length us, event | category | flops | bytes accessed | tf_op | source)
XLA Modules:
  0.0 51.5 jit_solution(14229156969427530231)
XLA Ops:
  0.0 0.0 copy-start.1
  0.0 0.0 copy-start
  0.0 0.0 copy-start.4
  0.0 0.0 copy-start.2
  0.0 0.0 copy-start.3
  0.0 0.0 copy-start.5
  0.0 0.8 %copy-done.5 = bf16[3,512]{1,0:T(4,128)(2,1)S(1)} copy-done((bf16[3,512]{1,0:T(4,128)(2,1)S(1)}, bf16[3,512]{1,0:T(4,128)(2,1)}, u32[]{:S(2)}) %copy-start.5) | copy-done | bytes 3096
  0.9 0.0 copy-start.6
  0.9 42.9 %shard_map.118.latent_ref = bf16[216,512]{1,0:T(8,128)(2,1)S(1)} custom-call(bf16[96,12,4,512]{3,2,1,0:T(4,128)(2,1)} %tokens.1, bf16[512,512]{1,0:T(8,128)(2,1)} %w_pq.1, bf16[512,512]{1,0:T(8,128)(2,1)} %w_pk.1, bf16[512,512]{1,0:T(8,128)(2,1)} %w_pv.1, bf16[512,512]{1,0:T(8,128)(2,1)} %w_po.1, bf16[3,512]{1,0:T(4,128)(2,1)S(1)} %copy-done.5), custom_call_target="tpu_custom_call" | custom-call | flops 8000000000 | bytes 100000000 | tf_op jit(solution)/shard_map/pallas_call | solution.py:415
  43.8 0.0 copy-done.1
  43.8 0.0 copy-done
  43.8 0.0 copy-done.4
  43.8 0.0 copy-done.2
  43.8 0.0 copy-done.3
  43.8 0.0 copy-done.6
  43.8 7.5 %shard_map.119 = bf16[6,12,3,512]{3,2,1,0:T(4,128)(2,1)} custom-call(bf16[216,512]{1,0:T(8,128)(2,1)S(1)} %shard_map.118.latent_ref, f32[2,512]{1,0:T(2,128)S(1)} %copy-done.6, bf16[512,512]{1,0:T(8,128)(2,1)S(1)} %copy-done.3, bf16[512,1024]{1,0:T(8,128)(2,1)S(1)} %copy-done.2, bf16[512,512]{1,0:T(8,128)(2,1)S(1)} %copy-done.4, ...), custom_call_target="tpu_custom_call" | custom-call | flops 2000000000 | bytes 7000000 | tf_op jit(solution)/shard_map/pallas_call | solution.py:463
Async XLA Ops:
  0.0 43.8 %copy-start.1 = (bf16[2048,512]{1,0:T(8,128)(2,1)S(1)}, bf16[2048,512]{1,0:T(8,128)(2,1)}, u32[]{:S(2)}) copy-start(bf16[2048,512]{1,0:T(8,128)(2,1)} %w_down.1) | copy-start | bytes 6291460
  0.0 43.8 %copy-start = (bf16[512,2048]{1,0:T(8,128)(2,1)S(1)}, bf16[512,2048]{1,0:T(8,128)(2,1)}, u32[]{:S(2)}) copy-start(bf16[512,2048]{1,0:T(8,128)(2,1)} %w_up.1) | copy-start | bytes 6291460
  0.0 43.8 %copy-start.4 = (bf16[512,512]{1,0:T(8,128)(2,1)S(1)}, bf16[512,512]{1,0:T(8,128)(2,1)}, u32[]{:S(2)}) copy-start(bf16[512,512]{1,0:T(8,128)(2,1)} %w_so.1) | copy-start | bytes 1572868
  0.0 43.8 %copy-start.2 = (bf16[512,1024]{1,0:T(8,128)(2,1)S(1)}, bf16[512,1024]{1,0:T(8,128)(2,1)}, u32[]{:S(2)}) copy-start(bf16[512,1024]{1,0:T(8,128)(2,1)} %w_skv.1) | copy-start | bytes 3145732
  0.0 43.8 %copy-start.3 = (bf16[512,512]{1,0:T(8,128)(2,1)S(1)}, bf16[512,512]{1,0:T(8,128)(2,1)}, u32[]{:S(2)}) copy-start(bf16[512,512]{1,0:T(8,128)(2,1)} %w_sq.1) | copy-start | bytes 1572868
  0.0 0.8 %copy-start.5 = (bf16[3,512]{1,0:T(4,128)(2,1)S(1)}, bf16[3,512]{1,0:T(4,128)(2,1)}, u32[]{:S(2)}) copy-start(bf16[3,512]{1,0:T(4,128)(2,1)} %lq_ref.1) | copy-start | bytes 9220
  0.9 43.0 %copy-start.6 = (f32[2,512]{1,0:T(2,128)S(1)}, f32[2,512]{1,0:T(2,128)}, u32[]{:S(2)}) copy-start(f32[2,512]{1,0:T(2,128)} %gains_ref.1) | copy-start | bytes 12292

commit v10 on v9

--- a/solution.py
+++ b/solution.py
@@ -184,7 +184,7 @@
             [rows[:, group * 256 : (group + 1) * 256].astype(F32), rest], axis=0
         )
 
-    lane_wide = lax.broadcasted_iota(jnp.int32, (BOTH, STATS), 1)
+    lane_part = lax.broadcasted_iota(jnp.int32, (PATCHES, STATS), 1)
 
     def products(half, k, src):
         index = half * RING + k
@@ -202,11 +202,10 @@
         if k + 2 < RING:
             send_tokens(half, k + 2)
 
-    def work(half, k):
-        slot = slot_of(half, k)
+    def sums(half, k, which):
         index = half * RING + k
         members = [
-            pl.ds(src * BOTH * LEVS + t, BOTH, stride=LEVS)
+            pl.ds((src * BOTH + which * PATCHES) * LEVS + t, PATCHES, stride=LEVS)
             for src in range(2)
             for t in range(LEVS)
         ]
@@ -214,26 +213,36 @@
         top = functools.reduce(jnp.maximum, scores)
         weights = [jnp.exp(score - top) for score in scores]
         total = sum(weights)
-        inverse = jnp.where(lane_wide < STATS // 2, 1.0 / total, 0.0)
+        inverse = jnp.where(lane_part < STATS // 2, 1.0 / total, 0.0)
+        at_p = 2 * half + which
         for n, weight in enumerate(weights):
-            p_scr[half, n * BOTH : (n + 1) * BOTH, :] = (weight * inverse).astype(BF16)
+            p_scr[at_p, n * PAD : n * PAD + PATCHES, :] = (weight * inverse).astype(BF16)
         stats = top + jnp.log(total)
-        kstat[index, 0:PATCHES, :] = stats[:PATCHES]
-        t_scr[half, 0:PATCHES, :] = stats[PATCHES:]
-        sstat[index] = fold(t_scr[half])
+        if which == 0:
+            kstat[index, 0:PATCHES, :] = stats
+        else:
+            t_scr[half, 0:PATCHES, :] = stats
+            sstat[index] = fold(t_scr[half])
         for at in range(0, LATENT * D, 256):
-            wide = dot(p_scr[half], ex_scr[:, at : at + 256])
+            wide = dot(p_scr[at_p], ex_scr[:, at : at + 256])
             sides = [
                 sum(
                     v_scr[index, (at % D) // 128 + side, member, :]
-                    * wide[n * BOTH : (n + 1) * BOTH, side * 128 : (side + 1) * 128]
+                    * wide[n * PAD : n * PAD + PATCHES, side * 128 : (side + 1) * 128]
                     for n, member in enumerate(members)
                 )
                 for side in range(2)
             ]
             here = jnp.concatenate(sides, axis=1)
-            keep[index, 0:PATCHES, at : at + 256] = here[:PATCHES]
-            pack(snum, index, at // 256, here[PATCHES:])
+            if which == 0:
+                keep[index, 0:PATCHES, at : at + 256] = here
+            else:
+                pack(snum, index, at // 256, here)
+
+    def work(half, k):
+        slot = slot_of(half, k)
+        index = half * RING + k
+        sums(half, k, 1)
         _, second = partners(half, slot)
         for src, dst, send, recv in (
             (snum, rnum, num_send, num_recv), (sstat, rstat, stat_send, stat_recv)
@@ -294,8 +303,11 @@
             products(half, k, 1)
         for half in (1, 0):
             work(half, k)
+        for half in (1, 0):
             if k > 0:
                 merge(half, k - 1)
+        for half in (1, 0):
+            sums(half, k, 0)
     for half in (1, 0):
         merge(half, RING - 1)
 
@@ -424,7 +436,7 @@
             pltpu.VMEM((STATS, LATENT * D), BF16),
             pltpu.VMEM((pieces, GATHERED, STATS), F32),
             pltpu.VMEM((pieces, D // 128, GATHERED, 128), F32),
-            pltpu.VMEM((2, GATHERED, STATS), BF16),
+            pltpu.VMEM((4, 2 * LEVS * PAD, STATS), BF16),
             pltpu.VMEM((RING * PAD, LATENT * D), F32),
             pltpu.VMEM((RING * PAD, STATS), F32),
             pltpu.VMEM((pieces, PAD, LATENT * D), F32),

time: 51.6 us -> 51.4 us (level)
  no operation moved by 1% of the time
where the time goes in v10:
time: 51.4 us; the launch traced here: 51.3 us
  Pallas kernels  50.2 us (98%)
  local copies, waits for them, and re-layouts  0.85 us (2%)
    pallas_call x1, Pallas kernels, body(): pl.pallas_call(gather_kernel, out_shape=jax.ShapeDtypeStruct((ROWS, D), B...  42.7 us
    pallas_call x1, Pallas kernels, body(): pl.pallas_call(window_kernel, out_shape=jax.ShapeDtypeStruct((WLAT, 2 * H...  7.51 us

profile of v10, /device:TPU:1, one launch (start us, length us, event | category | flops | bytes accessed | tf_op | source)
XLA Modules:
  0.0 51.3 jit_solution(15434986878984769403)
XLA Ops:
  0.0 0.0 copy-start.1
  0.0 0.0 copy-start
  0.0 0.0 copy-start.4
  0.0 0.0 copy-start.2
  0.0 0.0 copy-start.3
  0.0 0.0 copy-start.5
  0.0 0.8 %copy-done.5 = bf16[3,512]{1,0:T(4,128)(2,1)S(1)} copy-done((bf16[3,512]{1,0:T(4,128)(2,1)S(1)}, bf16[3,512]{1,0:T(4,128)(2,1)}, u32[]{:S(2)}) %copy-start.5) | copy-done | bytes 3096
  0.9 0.0 copy-start.6
  0.9 42.7 %shard_map.118.latent_ref = bf16[216,512]{1,0:T(8,128)(2,1)S(1)} custom-call(bf16[96,12,4,512]{3,2,1,0:T(4,128)(2,1)} %tokens.1, bf16[512,512]{1,0:T(8,128)(2,1)} %w_pq.1, bf16[512,512]{1,0:T(8,128)(2,1)} %w_pk.1, bf16[512,512]{1,0:T(8,128)(2,1)} %w_pv.1, bf16[512,512]{1,0:T(8,128)(2,1)} %w_po.1, bf16[3,512]{1,0:T(4,128)(2,1)S(1)} %copy-done.5), custom_call_target="tpu_custom_call" | custom-call | flops 8000000000 | bytes 100000000 | tf_op jit(solution)/shard_map/pallas_call | solution.py:427
  43.6 0.0 copy-done.1
  43.6 0.0 copy-done
  43.6 0.0 copy-done.4
  43.6 0.0 copy-done.2
  43.6 0.0 copy-done.3
  43.6 0.0 copy-done.6
  43.6 7.5 %shard_map.119 = bf16[6,12,3,512]{3,2,1,0:T(4,128)(2,1)} custom-call(bf16[216,512]{1,0:T(8,128)(2,1)S(1)} %shard_map.118.latent_ref, f32[2,512]{1,0:T(2,128)S(1)} %copy-done.6, bf16[512,512]{1,0:T(8,128)(2,1)S(1)} %copy-done.3, bf16[512,1024]{1,0:T(8,128)(2,1)S(1)} %copy-done.2, bf16[512,512]{1,0:T(8,128)(2,1)S(1)} %copy-done.4, ...), custom_call_target="tpu_custom_call" | custom-call | flops 2000000000 | bytes 7000000 | tf_op jit(solution)/shard_map/pallas_call | solution.py:475
Async XLA Ops:
  0.0 43.6 %copy-start.1 = (bf16[2048,512]{1,0:T(8,128)(2,1)S(1)}, bf16[2048,512]{1,0:T(8,128)(2,1)}, u32[]{:S(2)}) copy-start(bf16[2048,512]{1,0:T(8,128)(2,1)} %w_down.1) | copy-start | bytes 6291460
  0.0 43.6 %copy-start = (bf16[512,2048]{1,0:T(8,128)(2,1)S(1)}, bf16[512,2048]{1,0:T(8,128)(2,1)}, u32[]{:S(2)}) copy-start(bf16[512,2048]{1,0:T(8,128)(2,1)} %w_up.1) | copy-start | bytes 6291460
  0.0 43.6 %copy-start.4 = (bf16[512,512]{1,0:T(8,128)(2,1)S(1)}, bf16[512,512]{1,0:T(8,128)(2,1)}, u32[]{:S(2)}) copy-start(bf16[512,512]{1,0:T(8,128)(2,1)} %w_so.1) | copy-start | bytes 1572868
  0.0 43.6 %copy-start.2 = (bf16[512,1024]{1,0:T(8,128)(2,1)S(1)}, bf16[512,1024]{1,0:T(8,128)(2,1)}, u32[]{:S(2)}) copy-start(bf16[512,1024]{1,0:T(8,128)(2,1)} %w_skv.1) | copy-start | bytes 3145732
  0.0 43.6 %copy-start.3 = (bf16[512,512]{1,0:T(8,128)(2,1)S(1)}, bf16[512,512]{1,0:T(8,128)(2,1)}, u32[]{:S(2)}) copy-start(bf16[512,512]{1,0:T(8,128)(2,1)} %w_sq.1) | copy-start | bytes 1572868
  0.0 0.8 %copy-start.5 = (bf16[3,512]{1,0:T(4,128)(2,1)S(1)}, bf16[3,512]{1,0:T(4,128)(2,1)}, u32[]{:S(2)}) copy-start(bf16[3,512]{1,0:T(4,128)(2,1)} %lq_ref.1) | copy-start | bytes 9220
  0.9 42.8 %copy-start.6 = (f32[2,512]{1,0:T(2,128)S(1)}, f32[2,512]{1,0:T(2,128)}, u32[]{:S(2)}) copy-start(f32[2,512]{1,0:T(2,128)} %gains_ref.1) | copy-start | bytes 12292

commit v11 on v10

--- a/solution.py
+++ b/solution.py
@@ -301,7 +301,6 @@
             arrive(half, k)
         for half in (1, 0):
             products(half, k, 1)
-        for half in (1, 0):
             work(half, k)
         for half in (1, 0):
             if k > 0:

time: 51.4 us -> 51.3 us (level)
  no operation moved by 1% of the time
where the time goes in v11:
time: 51.3 us; the launch traced here: 51.2 us
  Pallas kernels  50.1 us (98%)
  local copies, waits for them, and re-layouts  0.85 us (2%)
    pallas_call x1, Pallas kernels, body(): pl.pallas_call(gather_kernel, out_shape=jax.ShapeDtypeStruct((ROWS, D), B...  42.6 us
    pallas_call x1, Pallas kernels, body(): pl.pallas_call(window_kernel, out_shape=jax.ShapeDtypeStruct((WLAT, 2 * H...  7.51 us

profile of v11, /device:TPU:1, one launch (start us, length us, event | category | flops | bytes accessed | tf_op | source)
XLA Modules:
  0.0 51.2 jit_solution(911002718210241221)
XLA Ops:
  0.0 0.0 copy-start.1
  0.0 0.0 copy-start
  0.0 0.0 copy-start.4
  0.0 0.0 copy-start.2
  0.0 0.0 copy-start.3
  0.0 0.0 copy-start.5
  0.0 0.8 %copy-done.5 = bf16[3,512]{1,0:T(4,128)(2,1)S(1)} copy-done((bf16[3,512]{1,0:T(4,128)(2,1)S(1)}, bf16[3,512]{1,0:T(4,128)(2,1)}, u32[]{:S(2)}) %copy-start.5) | copy-done | bytes 3096
  0.9 0.0 copy-start.6
  0.9 42.6 %shard_map.118.latent_ref = bf16[216,512]{1,0:T(8,128)(2,1)S(1)} custom-call(bf16[96,12,4,512]{3,2,1,0:T(4,128)(2,1)} %tokens.1, bf16[512,512]{1,0:T(8,128)(2,1)} %w_pq.1, bf16[512,512]{1,0:T(8,128)(2,1)} %w_pk.1, bf16[512,512]{1,0:T(8,128)(2,1)} %w_pv.1, bf16[512,512]{1,0:T(8,128)(2,1)} %w_po.1, bf16[3,512]{1,0:T(4,128)(2,1)S(1)} %copy-done.5), custom_call_target="tpu_custom_call" | custom-call | flops 8000000000 | bytes 100000000 | tf_op jit(solution)/shard_map/pallas_call | solution.py:426
  43.5 0.0 copy-done.1
  43.5 0.0 copy-done
  43.5 0.0 copy-done.4
  43.5 0.0 copy-done.2
  43.5 0.0 copy-done.3
  43.5 0.0 copy-done.6
  43.5 7.5 %shard_map.119 = bf16[6,12,3,512]{3,2,1,0:T(4,128)(2,1)} custom-call(bf16[216,512]{1,0:T(8,128)(2,1)S(1)} %shard_map.118.latent_ref, f32[2,512]{1,0:T(2,128)S(1)} %copy-done.6, bf16[512,512]{1,0:T(8,128)(2,1)S(1)} %copy-done.3, bf16[512,1024]{1,0:T(8,128)(2,1)S(1)} %copy-done.2, bf16[512,512]{1,0:T(8,128)(2,1)S(1)} %copy-done.4, ...), custom_call_target="tpu_custom_call" | custom-call | flops 2000000000 | bytes 7000000 | tf_op jit(solution)/shard_map/pallas_call | solution.py:474
Async XLA Ops:
  0.0 43.5 %copy-start.1 = (bf16[2048,512]{1,0:T(8,128)(2,1)S(1)}, bf16[2048,512]{1,0:T(8,128)(2,1)}, u32[]{:S(2)}) copy-start(bf16[2048,512]{1,0:T(8,128)(2,1)} %w_down.1) | copy-start | bytes 6291460
  0.0 43.5 %copy-start = (bf16[512,2048]{1,0:T(8,128)(2,1)S(1)}, bf16[512,2048]{1,0:T(8,128)(2,1)}, u32[]{:S(2)}) copy-start(bf16[512,2048]{1,0:T(8,128)(2,1)} %w_up.1) | copy-start | bytes 6291460
  0.0 43.5 %copy-start.4 = (bf16[512,512]{1,0:T(8,128)(2,1)S(1)}, bf16[512,512]{1,0:T(8,128)(2,1)}, u32[]{:S(2)}) copy-start(bf16[512,512]{1,0:T(8,128)(2,1)} %w_so.1) | copy-start | bytes 1572868
  0.0 43.5 %copy-start.2 = (bf16[512,1024]{1,0:T(8,128)(2,1)S(1)}, bf16[512,1024]{1,0:T(8,128)(2,1)}, u32[]{:S(2)}) copy-start(bf16[512,1024]{1,0:T(8,128)(2,1)} %w_skv.1) | copy-start | bytes 3145732
  0.0 43.5 %copy-start.3 = (bf16[512,512]{1,0:T(8,128)(2,1)S(1)}, bf16[512,512]{1,0:T(8,128)(2,1)}, u32[]{:S(2)}) copy-start(bf16[512,512]{1,0:T(8,128)(2,1)} %w_sq.1) | copy-start | bytes 1572868
  0.0 0.8 %copy-start.5 = (bf16[3,512]{1,0:T(4,128)(2,1)S(1)}, bf16[3,512]{1,0:T(4,128)(2,1)}, u32[]{:S(2)}) copy-start(bf16[3,512]{1,0:T(4,128)(2,1)} %lq_ref.1) | copy-start | bytes 9220
  0.9 42.7 %copy-start.6 = (f32[2,512]{1,0:T(2,128)S(1)}, f32[2,512]{1,0:T(2,128)}, u32[]{:S(2)}) copy-start(f32[2,512]{1,0:T(2,128)} %gains_ref.1) | copy-start | bytes 12292
